TPU v7x, 512 devices: a whole 4x8x8 slice. The times are simulated.
512 devices in a mesh: section: 8 (over z_lo, core), slab: 64 (over x, z_hi, y).
Axes of the slice: x: 4, y: 8, z: 8 (z_hi: 2, z_lo: 4; z = z_hi * 4 + z_lo), core: 2. Of those that a mesh axis runs over, the one named last changes fastest.
Arguments:
- saved_in: bfloat16 [8, 128, 32, 8, 128], P('section', 'slab'), may hold values from -6 to 6
- saved_out: bfloat16 [8, 128, 32, 8, 128], P('section', 'slab'), as said below
- weights: bfloat16 [8, 27, 128, 128], P('section'), may hold values from -0.15625 to 0.15625
- cotangent: bfloat16 [128, 32, 8, 128], P('slab'), may hold values from -6 to 6
Outputs:
- act_grads: bfloat16 [8, 128, 32, 8, 128], P('section', 'slab')
- kernel_grads: float32 [8, 27, 128, 128], P('section')
- bias_grads: float32 [8, 128], P('section')
Inputs may be any that keep to these rules, and one draw needn't show every extreme that they name: `saved_out`: every entry is zero or positive.
All inputs are finite; a program needn't handle non-finite values.
Results may differ from a plain program's by a relative error of at most 0.015.
Values may be sent and summed in bfloat16 or wider, within the bound.
A program may use at most 64 MiB of HBM per device.

v0:
```python
import math

import jax
import jax.numpy as jnp
from jax import lax
from jax.sharding import PartitionSpec as P


def padded_2(block, sides, width):
    for axis, dim in sides:
        count = lax.axis_size(axis)
        forward = [(i, i + 1) for i in range(count - 1)]
        backward = [(target, source) for source, target in forward]
        low = lax.ppermute(
            lax.slice_in_dim(block, block.shape[dim] - width, None, axis=dim), axis, forward
        )
        high = lax.ppermute(lax.slice_in_dim(block, 0, width, axis=dim), axis, backward)
        block = jnp.concatenate([low, block, high], axis=dim)
    return block


def from_behind(block, axis, distance):
    devices = range(lax.axis_size(axis))
    route = [(i - distance, i) for i in devices if i - distance in devices]
    return lax.ppermute(block, axis, route)


def stacked_depth(padded, depth):
    return jnp.concatenate(
        [padded[:, :, offset : offset + depth, :] for offset in range(3)], axis=-1
    )


def pad_sides(block):
    return jnp.pad(block, ((0, 0), (1, 1), (1, 1), (0, 0)))


def input_grad(stacked, flipped, rows_y, cells_x):
    breadth = stacked.shape[-1]
    summed = jnp.zeros((rows_y * cells_x * stacked.shape[2], flipped.shape[-1]), jnp.float32)
    for offset_y in range(3):
        for offset_x in range(3):
            window = stacked[offset_y : offset_y + rows_y, offset_x : offset_x + cells_x].reshape(
                -1, breadth
            )
            summed = summed + jnp.dot(
                window, flipped[offset_y, offset_x], preferred_element_type=jnp.float32
            )
    return summed


def kernel_grad(stacked, masked, rows_y, cells_x):
    breadth = stacked.shape[-1]
    flattened = masked.reshape(-1, masked.shape[-1])
    blocks = []
    for offset_y in range(3):
        for offset_x in range(3):
            window = stacked[offset_y : offset_y + rows_y, offset_x : offset_x + cells_x].reshape(
                -1, breadth
            )
            blocks.append(
                lax.dot_general(
                    window, flattened, (((0,), (0,)), ((), ())), preferred_element_type=jnp.float32
                )
            )
    return jnp.stack(blocks).reshape(27, breadth // 3, flattened.shape[-1])


def local(saved_in, saved_out, weights, cotangent):
    sections = lax.axis_size("section")
    half_sections = sections // 2
    my_section = lax.axis_index("section")
    layer_input = saved_in[0]
    live_mask = saved_out[0] > 0
    kernel = weights[0]
    rows_y, cells_x, cells_z, channels = layer_input.shape
    flipped = (
        kernel.reshape(3, 3, 3, channels, channels)[::-1, ::-1, ::-1]
        .transpose(0, 1, 2, 4, 3)
        .reshape(3, 3, 3 * channels, channels)
    )
    norm_factor = 1.0 / math.sqrt(rows_y * lax.axis_size("slab") * cells_x * cells_z)
    input_rim = padded_2(layer_input, (("slab", 0),), 1)
    input_stack = stacked_depth(pad_sides(input_rim), cells_z)

    def backward_data(padded):
        return input_grad(stacked_depth(padded, cells_z), flipped, rows_y, cells_x).reshape(
            rows_y, cells_x, cells_z, channels
        )

    def no_data(padded):
        return jnp.zeros((rows_y, cells_x, cells_z, channels), jnp.float32)

    incoming = cotangent
    zero_block = jnp.zeros_like(cotangent)
    skip_grad = zero_block
    act_grad = zero_block
    kept_grad = zero_block
    for turn_number in range(sections):
        active = my_section == sections - 1 - turn_number
        masked = jnp.where(live_mask, incoming, zero_block)
        grad_rim = padded_2(masked, (("slab", 0),), 1)
        input_part = lax.cond(active, backward_data, no_data, pad_sides(grad_rim))
        outgoing = (input_part + skip_grad.astype(jnp.float32)).astype(jnp.bfloat16)
        act_grad = jnp.where(active, outgoing, act_grad)
        kept_grad = jnp.where(active, masked, kept_grad)
        if turn_number == half_sections - 1:
            mirrored = from_behind(act_grad, "section", -half_sections)
            skip_grad = jnp.where(my_section < half_sections, mirrored, zero_block)
        if turn_number < sections - 1:
            incoming = from_behind(outgoing, "section", -1)
    kernel_part = kernel_grad(input_stack, kept_grad, rows_y, cells_x) * norm_factor
    bias_part = jnp.sum(kept_grad, axis=(0, 1, 2), dtype=jnp.float32) * norm_factor
    kernel_sum = kernel_part
    bias_sum = bias_part
    kernel_sum, bias_sum = lax.psum((kernel_sum, bias_sum), "slab")
    return (act_grad[None], kernel_sum[None], bias_sum[None])


def solution(mesh):
    placed = (
        P("section", "slab", None, None, None),
        P("section", "slab", None, None, None),
        P("section", None, None, None),
        P("slab", None, None, None),
    )
    return jax.shard_map(
        local,
        mesh=mesh,
        in_specs=placed,
        out_specs=(
            P("section", "slab", None, None, None),
            P("section", None, None, None),
            P("section", None),
        ),
        check_vma=False,
    )
```

profile of v0, /device:TPU:8, one launch (start us, length us, event | category | flops | bytes accessed | tf_op | source)
XLA Modules:
  0.0 1030.0 jit_solution(13969159940464421414)
XLA Ops:
  8.2 7.7 collective-permute-start.1
  17.9 2.0 copy.7
  20.0 2.1 collective-permute-done
  23.5 1.9 collective-permute-done.2
  27.4 3.9 collective-permute-start.3
  31.7 1.9 collective-permute-done.3
  35.0 1.9 collective-permute-done.5
  38.9 3.9 collective-permute-start.6
  46.4 2.3 collective-permute-done.8
  50.7 3.9 collective-permute-start.9
  55.0 1.9 collective-permute-done.9
  58.3 3.8 collective-permute-done.11
  64.1 4.4 collective-permute-start.12
  70.7 17.7 %collective-permute-done.14 = bf16[2,32,8,128]{3,2,1,0:T(8,128)(2,1)S(1)} collective-permute-done((bf16[2,32,8,128]{3,2,1,0:T(8,128)(2,1)S(1)}, bf16[2,32,8,128]{3,2,1,0:T(8,128)(2,1)S(1)}, u32[]{:S(2)}, u32[]{:S(2)}) %collective-permute-start.14) | collective-permute-done | bytes 131104 | tf_op jit(solution)/shard_map/ppermute | solution.py:25
  93.6 5.1 collective-permute-start.16
  100.7 5.7 collective-permute-start.24
  108.4 3.5 collective-permute-done.18
  113.9 5.8 collective-permute-start.19
  123.2 8.9 collective-permute-done.21
  138.5 10.3 collective-permute-start.22
  148.8 231.9 %psum.15 = f32[1,128]{1,0:T(1,128)} all-reduce(f32[1,128]{1,0:T(1,128)S(1)} %multiply_bitcast_fusion), channel_id=1, replica_groups=mesh['section'=8,'slab'=64] {'slab'}, use_global_device_ids=true, to_apply=%region_18.19 | all-reduce | flops 128 | bytes 1024 | tf_op jit(solution)/shard_map/psum | solution.py:116
  380.7 3.1 conditional.15
  384.6 635.7 %all-reduce.11.cloned.1.call-done = f32[1,27,128,128]{3,2,1,0:T(8,128)} async-done(((f32[1,27,128,128]{3,2,1,0:T(8,128)}), f32[1,27,128,128]{3,2,1,0:T(8,128)}) %all-reduce.11.cloned.1.call-update) | async-done | bytes 1769488 | tf_op jit(solution)/shard_map/psum | solution.py:116
  1020.3 2.9 copy.75
  (121 shorter events, 45.9 us)
Async XLA Ops:
  7.2 1013.1 %all-reduce.11.cloned.1.call-start = ((), (), s32[]{:S(2)}) async-start(), calls=%async_computation | async-start | bytes 3538944 | tf_op jit(solution)/shard_map/psum | solution.py:116
  8.2 11.8 %collective-permute-start.1 = (bf16[1,32,8,128]{3,2,1,0:T(8,128)(2,1)S(1)}, bf16[1,32,8,128]{3,2,1,0:T(8,128)(2,1)S(1)}, u32[]{:S(2)}, u32[]{:S(2)}) collective-permute-start(bf16[1,32,8,128]{3,2,1,0:T(8,128)(2,1)S(1)} %get-tuple-element.218), channel_id=1, source_target_pairs={{1,0},{2,1},{3,2},{4,3},{5,4},{6,5},{7,6},{8,7},{9,8},{10,9},{11,1... | collective-permute-start | bytes 196616 | tf_op jit(solution)/shard_map/ppermute | solution.py:17
  16.0 6.2 collective-permute-start
  25.5 6.2 collective-permute-start.4
  27.4 6.2 collective-permute-start.3
  37.0 6.2 collective-permute-start.7
  38.9 6.2 collective-permute-start.6
  45.1 3.6 collective-permute-start.8
  48.8 6.2 collective-permute-start.10
  50.7 6.2 collective-permute-start.9
  57.0 5.1 collective-permute-start.11
  62.2 7.7 collective-permute-start.13
  64.1 6.3 collective-permute-start.12
  68.6 19.8 %collective-permute-start.14 = (bf16[2,32,8,128]{3,2,1,0:T(8,128)(2,1)S(1)}, bf16[2,32,8,128]{3,2,1,0:T(8,128)(2,1)S(1)}, u32[]{:S(2)}, u32[]{:S(2)}) collective-permute-start(bf16[2,32,8,128]{3,2,1,0:T(8,128)(2,1)S(1)} %select_select_fusion.1), channel_id=1, source_target_pairs={{256,0},{320,64},{384,128},{448,192},{257,1},{321,65},{385,129},{4... | collective-permute-start | bytes 393224 | tf_op jit(solution)/shard_map/ppermute | solution.py:25
  91.7 14.7 %collective-permute-start.17 = (bf16[1,32,8,128]{3,2,1,0:T(8,128)(2,1)S(1)}, bf16[1,32,8,128]{3,2,1,0:T(8,128)(2,1)S(1)}, u32[]{:S(2)}, u32[]{:S(2)}) collective-permute-start(bf16[1,32,8,128]{3,2,1,0:T(8,128)(2,1)S(1)} %get-tuple-element.208), channel_id=1, source_target_pairs={{1,0},{2,1},{3,2},{4,3},{5,4},{6,5},{7,6},{8,7},{9,8},{10,9},{11,1... | collective-permute-start | bytes 196616 | tf_op jit(solution)/shard_map/ppermute | solution.py:17
  93.6 12.8 %collective-permute-start.16 = (bf16[1,32,8,128]{3,2,1,0:T(8,128)(2,1)S(1)}, bf16[1,32,8,128]{3,2,1,0:T(8,128)(2,1)S(1)}, u32[]{:S(2)}, u32[]{:S(2)}) collective-permute-start(bf16[1,32,8,128]{3,2,1,0:T(8,128)(2,1)S(1)} %get-tuple-element.207), channel_id=1, source_target_pairs={{0,1},{1,2},{2,3},{3,4},{4,5},{5,6},{6,7},{7,8},{8,9},{9,10},{10,1... | collective-permute-start | bytes 196616 | tf_op jit(solution)/shard_map/ppermute | solution.py:14
  98.8 9.1 collective-permute-start.25
  100.7 7.6 collective-permute-start.24
  106.6 5.3 collective-permute-start.18
  112.0 8.1 collective-permute-start.20
  113.9 7.7 collective-permute-start.19
  121.8 10.3 %collective-permute-start.21 = (bf16[2,32,8,128]{3,2,1,0:T(8,128)(2,1)S(1)}, bf16[2,32,8,128]{3,2,1,0:T(8,128)(2,1)S(1)}, u32[]{:S(2)}, u32[]{:S(2)}) collective-permute-start(bf16[2,32,8,128]{3,2,1,0:T(8,128)(2,1)S(1)} %fusion.182), channel_id=1, source_target_pairs={{64,0},{128,64},{192,128},{256,192},{320,256},{384,320},{448,384},... | collective-permute-start | bytes 393224 | tf_op jit(solution)/shard_map/ppermute | solution.py:25
  136.6 244.1 %collective-permute-start.23 = (bf16[1,32,8,128]{3,2,1,0:T(8,128)(2,1)S(1)}, bf16[1,32,8,128]{3,2,1,0:T(8,128)(2,1)S(1)}, u32[]{:S(2)}, u32[]{:S(2)}) collective-permute-start(bf16[1,32,8,128]{3,2,1,0:T(8,128)(2,1)S(1)} %get-tuple-element.204), channel_id=1, source_target_pairs={{1,0},{2,1},{3,2},{4,3},{5,4},{6,5},{7,6},{8,7},{9,8},{10,9},{11,1... | collective-permute-start | bytes 196616 | tf_op jit(solution)/shard_map/ppermute | solution.py:17
  138.5 242.2 %collective-permute-start.22 = (bf16[1,32,8,128]{3,2,1,0:T(8,128)(2,1)S(1)}, bf16[1,32,8,128]{3,2,1,0:T(8,128)(2,1)S(1)}, u32[]{:S(2)}, u32[]{:S(2)}) collective-permute-start(bf16[1,32,8,128]{3,2,1,0:T(8,128)(2,1)S(1)} %get-tuple-element.203), channel_id=1, source_target_pairs={{0,1},{1,2},{2,3},{3,4},{4,5},{5,6},{6,7},{7,8},{8,9},{9,10},{10,1... | collective-permute-start | bytes 196616 | tf_op jit(solution)/shard_map/ppermute | solution.py:14
  (10 other events, 49.1 us)
Sparse Core Ops, SparseCore 0:
  136.7 883.5 all-reduce.10
where the time goes:
time: 1030 us
  waiting for transfers between devices  689 us (67%)
  blocking collectives  232 us (23%)
  starting transfers between devices  78.5 us (8%)
  between operations  14.8 us (1%)
    psum x1, waiting for transfers between devices, local(): kernel_sum, bias_sum = lax.psum((kernel_sum, bias_sum), 'slab')  636 us
    psum x1, blocking collectives, local(): kernel_sum, bias_sum = lax.psum((kernel_sum, bias_sum), 'slab')  232 us
    ppermute x9, starting transfers between devices, padded_2(): lax.ppermute(lax.slice_in_dim(block, block.shape[dim] - width, None, axis...  45.1 us
    ppermute x8, waiting for transfers between devices, from_behind(): return lax.ppermute(block, axis, route)  42 us
    ppermute x9, starting transfers between devices, padded_2(): lax.ppermute(lax.slice_in_dim(block, 0, width, axis=dim), axis, backward)  23.1 us
  transfers between devices with their start and end apart: 27, of which 20 were waited for; matrix products, arithmetic and copies ran while one was open for 1% of the time, Pallas kernels for 0%

commit v1 on v0

v1 whole, which is shorter than its diff:
```python
import math

import jax
import jax.numpy as jnp
from jax import lax
from jax.experimental import pallas as pl
from jax.experimental.pallas import tpu as pltpu
from jax.sharding import PartitionSpec as P

MESH = pl.DeviceIdType.MESH
F32 = jnp.float32
BF16 = jnp.bfloat16

RUN = 8
GROUPS = 8
CHUNK = 432
PART = 448


def kernel(
    si_ref, so_ref, w_ref, cot_ref,
    act_ref, kg_ref, bias_ref,
    inc, so6, act6, skip6, s0, s1, wst, sit, kgp, rsb, p2b, agb,
    halo_send, halo_recv, inc_send, inc_recv, skip_send, skip_recv,
    rs_send, rs_recv, p2_send, p2_recv, ag_send, ag_recv,
):
    sec = lax.axis_index("section")
    j = lax.axis_index("slab")
    n_sec = lax.axis_size("section")
    n_slab = lax.axis_size("slab")
    y = lax.rem(j, RUN)
    g = lax.div(j, RUN)
    odd = lax.rem(sec, 2) == 1
    even = lax.rem(sec, 2) == 0
    has_low = j > 0
    has_high = j < n_slab - 1
    top = sec == n_sec - 1

    def signal(s, t):
        pl.semaphore_signal(barrier, inc=1, device_id=(s, t), device_id_type=MESH)

    barrier = pltpu.get_barrier_semaphore()
    for d in range(1, RUN):
        signal(sec, g * RUN + lax.rem(y + d, RUN))
    for d in range(1, GROUPS):
        signal(sec, lax.rem(g + d, GROUPS) * RUN + y)

    @pl.when(jnp.logical_and(has_low, y == 0))
    def _():
        signal(sec, j - 1)

    @pl.when(jnp.logical_and(has_high, y == RUN - 1))
    def _():
        signal(sec, j + 1)

    @pl.when(sec > 0)
    def _():
        signal(sec - 1, j)

    @pl.when(jnp.logical_not(top))
    def _():
        signal(sec + 1, j)

    @pl.when(jnp.logical_and(even, jnp.logical_and(sec > 0, has_low)))
    def _():
        signal(sec - 1, j - 1)

    @pl.when(jnp.logical_and(even, jnp.logical_and(sec > 0, has_high)))
    def _():
        signal(sec - 1, j + 1)

    @pl.when(jnp.logical_and(odd, jnp.logical_and(jnp.logical_not(top), has_low)))
    def _():
        signal(sec + 1, j - 1)

    @pl.when(jnp.logical_and(odd, jnp.logical_and(jnp.logical_not(top), has_high)))
    def _():
        signal(sec + 1, j + 1)

    @pl.when(sec >= 4)
    def _():
        signal(sec - 4, j)

    @pl.when(sec < 4)
    def _():
        signal(sec + 4, j)

    def one(cond):
        return jnp.where(cond, 1, 0)

    diagonal = jnp.logical_or(
        jnp.logical_and(even, sec > 0), jnp.logical_and(odd, jnp.logical_not(top))
    )
    expected = (
        RUN - 1 + GROUPS - 1 + 1
        + one(jnp.logical_and(has_low, y == 0))
        + one(jnp.logical_and(has_high, y == RUN - 1))
        + one(sec > 0)
        + one(jnp.logical_not(top))
        + one(jnp.logical_and(diagonal, has_low))
        + one(jnp.logical_and(diagonal, has_high))
    )

    so = so_ref[...]
    so6[2:4] = so

    @pl.when(top)
    def _():
        so6[2:4] = jnp.where(so.astype(F32) > 0, cot_ref[...].astype(F32), 0.0).astype(BF16)

    @pl.when(jnp.logical_not(has_low))
    def _():
        so6[0:2] = jnp.zeros((2, 256, 128), BF16)

        @pl.when(odd)
        def _():
            inc[0:2] = jnp.zeros((2, 256, 128), BF16)

    @pl.when(jnp.logical_not(has_high))
    def _():
        so6[4:6] = jnp.zeros((2, 256, 128), BF16)

        @pl.when(odd)
        def _():
            inc[4:6] = jnp.zeros((2, 256, 128), BF16)

    pl.semaphore_wait(barrier, expected)

    def remote(src, dst, ss, rs, s, t):
        return pltpu.make_async_remote_copy(
            src_ref=src, dst_ref=dst, send_sem=ss, recv_sem=rs,
            device_id=(s, t), device_id_type=MESH,
        )

    def halo(low):
        own = so6.at[2:4]
        if low:
            return remote(own, so6.at[4:6], halo_send.at[0], halo_recv.at[0], sec, j - 1)
        return remote(own, so6.at[0:2], halo_send.at[1], halo_recv.at[1], sec, j + 1)

    @pl.when(has_low)
    def _():
        halo(True).start()

    @pl.when(has_high)
    def _():
        halo(False).start()

    def turn(c, carry):
        k = c
        tile = w_ref[k].astype(F32)
        wst[lax.div(k, 3), pl.ds(pl.multiple_of(lax.rem(k, 3) * 128, 128), 128), :] = tile.T.astype(BF16)
        return carry

    lax.fori_loop(0, 27, turn, 0)
    for r in range(4):
        sit[:, r * 128:(r + 1) * 128] = si_ref[
            r // 2, (r % 2) * 128:(r % 2) * 128 + 128
        ].astype(F32).T.astype(BF16)
    for r in range(6):
        s1[r, 0:16] = jnp.zeros((16, 384), BF16)
        s1[r, 256:272] = jnp.zeros((16, 384), BF16)

    @pl.when(has_low)
    def _():
        halo(False).wait_recv()

    @pl.when(has_high)
    def _():
        halo(True).wait_recv()

    def to_inc(which):
        own = act6.at[2:4]
        if which == 0:
            return remote(own, inc.at[2:4], inc_send.at[0], inc_recv.at[0], sec - 1, j)
        if which == 1:
            return remote(own, inc.at[4:6], inc_send.at[1], inc_recv.at[1], sec - 1, j - 1)
        if which == 2:
            return remote(own, inc.at[0:2], inc_send.at[2], inc_recv.at[2], sec - 1, j + 1)
        return remote(act6.at[1:5], inc.at[1:5], inc_send.at[0], inc_recv.at[3], sec - 1, j)

    def to_skip(rows):
        if rows == 4:
            return remote(act6.at[1:5], skip6.at[1:5], skip_send, skip_recv.at[0], sec - 4, j)
        return remote(act6.at[2:4], skip6.at[2:4], skip_send, skip_recv.at[1], sec - 4, j)

    @pl.when(jnp.logical_and(odd, jnp.logical_not(top)))
    def _():
        to_inc(0).wait_recv()

        @pl.when(has_high)
        def _():
            to_inc(1).wait_recv()

        @pl.when(has_low)
        def _():
            to_inc(2).wait_recv()

    @pl.when(even)
    def _():
        to_inc(3).wait_recv()

    depth = lax.rem(lax.broadcasted_iota(jnp.int32, (256, 128), 0), 8)

    def stack_row(r, carry):
        held = so6[r].astype(F32)
        arrived = jnp.where(held > 0, inc[r].astype(F32), 0.0)
        m = jnp.where(top, held, arrived)
        up = jnp.where(depth == 7, 0.0, pltpu.roll(m, 255, 0)).astype(BF16)
        down = jnp.where(depth == 0, 0.0, pltpu.roll(m, 1, 0)).astype(BF16)
        m = m.astype(BF16)
        s0[r, :, 0:128] = up
        s0[r, :, 128:256] = m
        s0[r, :, 256:384] = down
        s1[r, 8:264, 0:128] = up
        s1[r, 8:264, 128:256] = m
        s1[r, 8:264, 256:384] = down
        return carry

    @pl.when(odd)
    def _():
        lax.fori_loop(0, 6, stack_row, 0)

    @pl.when(even)
    def _():
        lax.fori_loop(1, 5, stack_row, 0)

    def shifted(r, dx):
        if dx == 0:
            return s0[r]
        if dx == 1:
            return s1[r, 0:256]
        return s1[r, 16:272]

    def conv_row(r, carry):
        acc = jnp.zeros((256, 128), F32)
        for dy in (-1, 0, 1):
            for dx in (-1, 0, 1):
                acc = acc + jnp.dot(
                    shifted(r - dy, dx), wst[3 * (dy + 1) + dx + 1], preferred_element_type=F32
                )
        out = jnp.where(sec < 4, acc + skip6[r].astype(F32), acc)
        act6[r] = out.astype(BF16)
        return carry

    def conv():
        @pl.when(jnp.logical_and(sec < 4, odd))
        def _():
            to_skip(4).wait_recv()

        @pl.when(jnp.logical_and(sec < 4, even))
        def _():
            to_skip(2).wait_recv()

        @pl.when(odd)
        def _():
            lax.fori_loop(1, 5, conv_row, 0)

        @pl.when(even)
        def _():
            lax.fori_loop(2, 4, conv_row, 0)

    @pl.when(sec > 0)
    def _():
        conv()

        @pl.when(odd)
        def _():
            to_inc(3).start()

        @pl.when(even)
        def _():
            to_inc(0).start()

            @pl.when(has_low)
            def _():
                to_inc(1).start()

            @pl.when(has_high)
            def _():
                to_inc(2).start()

        @pl.when(jnp.logical_and(sec >= 4, odd))
        def _():
            to_skip(4).start()

        @pl.when(jnp.logical_and(sec >= 4, even))
        def _():
            to_skip(2).start()

    for dy in (-1, 0, 1):
        for dx in (-1, 0, 1):
            rhs = jnp.concatenate([shifted(2 - dy, dx), shifted(3 - dy, dx)], axis=0)
            block = jnp.dot(sit[...], rhs, preferred_element_type=F32).astype(BF16)
            for dz in range(3):
                row = (9 * (dy + 1) + 3 * (dx + 1) + dz) * 128
                lo = row
                while lo < row + 128:
                    c = lo // CHUNK
                    hi = min(row + 128, (c + 1) * CHUNK)
                    kgp[c, lo - c * CHUNK:hi - c * CHUNK] = block[
                        lo - row:hi - row, dz * 128:(dz + 1) * 128
                    ]
                    lo = hi
    m = s0[2, :, 128:256].astype(F32) + s0[3, :, 128:256].astype(F32)

    def split(total):
        first = total.astype(BF16).astype(F32)
        rows = lax.broadcasted_iota(jnp.int32, (16, 128), 0)
        both = jnp.where(rows == 0, first, jnp.where(rows == 1, total - first, 0.0))
        return both.astype(BF16)

    bias_rows = split(jnp.sum(m, axis=0, keepdims=True))
    for c in range(RUN):
        kgp[c, CHUNK:PART] = bias_rows

    def rs(d):
        to = lax.rem(y + d, RUN)
        return remote(kgp.at[to], rsb.at[d], rs_send.at[d], rs_recv.at[d], sec, g * RUN + to)

    for d in range(1, RUN):
        rs(d).start()

    @pl.when(sec == 0)
    def _():
        conv()

    for d in range(1, RUN):
        rs(d).wait_recv()

    def piece(i, count):
        return pl.ds(pl.multiple_of(i * count, count), count)

    def add_run(i, carry):
        rows = piece(i, 48)
        total = kgp[y, rows].astype(F32)
        for d in range(1, RUN):
            total = total + rsb[d, rows].astype(F32)
        p2b[g, rows] = total.astype(BF16)
        return carry

    lax.fori_loop(0, CHUNK // 48, add_run, 0)
    total = kgp[y, CHUNK:PART].astype(F32)
    for d in range(1, RUN):
        total = total + rsb[d, CHUNK:PART].astype(F32)
    p2b[g, CHUNK:PART] = split(jnp.sum(total, axis=0, keepdims=True))

    def p2(d):
        to = lax.rem(g + d, GROUPS)
        return remote(p2b.at[g], p2b.at[g], p2_send.at[d], p2_recv.at[d], sec, to * RUN + y)

    def p2_in(d):
        source = lax.rem(g + GROUPS - d, GROUPS)
        return remote(p2b.at[source], p2b.at[source], p2_send.at[d], p2_recv.at[d], sec, source * RUN + y)

    for d in range(1, GROUPS):
        p2(d).start()
    for d in range(1, GROUPS):
        p2_in(d).wait_recv()

    def add_groups(i, carry):
        rows = piece(i, 48)
        total = p2b[0, rows].astype(F32)
        for d in range(1, GROUPS):
            total = total + p2b[d, rows].astype(F32)
        agb[y, rows] = total.astype(BF16)
        return carry

    lax.fori_loop(0, CHUNK // 48, add_groups, 0)

    def ag(d):
        to = lax.rem(y + d, RUN)
        return remote(agb.at[y], agb.at[y], ag_send.at[d], ag_recv.at[d], sec, g * RUN + to)

    def ag_in(d):
        source = lax.rem(y + RUN - d, RUN)
        return remote(agb.at[source], agb.at[source], ag_send.at[d], ag_recv.at[d], sec, g * RUN + source)

    for d in range(1, RUN):
        ag(d).start()

    total = p2b[0, CHUNK:PART].astype(F32)
    for d in range(1, GROUPS):
        total = total + p2b[d, CHUNK:PART].astype(F32)
    bias_ref[...] = jnp.broadcast_to(jnp.sum(total, axis=0, keepdims=True), (8, 128))
    act_ref[...] = act6[2:4]

    @pl.when(has_low)
    def _():
        halo(True).wait_send()

    @pl.when(has_high)
    def _():
        halo(False).wait_send()

    @pl.when(jnp.logical_and(sec > 0, odd))
    def _():
        to_inc(3).wait_send()

    @pl.when(jnp.logical_and(sec > 0, even))
    def _():
        to_inc(0).wait_send()

        @pl.when(has_low)
        def _():
            to_inc(1).wait_send()

        @pl.when(has_high)
        def _():
            to_inc(2).wait_send()

    @pl.when(jnp.logical_and(sec >= 4, odd))
    def _():
        to_skip(4).wait_send()

    @pl.when(jnp.logical_and(sec >= 4, even))
    def _():
        to_skip(2).wait_send()

    for d in range(1, RUN):
        rs(d).wait_send()
    for d in range(1, GROUPS):
        p2(d).wait_send()
    for d in range(1, RUN):
        ag(d).wait_send()
    for d in range(1, RUN):
        ag_in(d).wait_recv()
    kg_ref[...] = agb[...]


def local(saved_in, saved_out, weights, cotangent):
    rows_y, cells_x, cells_z, channels = cotangent.shape
    norm_factor = 1.0 / math.sqrt(rows_y * lax.axis_size("slab") * cells_x * cells_z)
    flat = (rows_y, cells_x * cells_z, channels)
    vmem = pl.BlockSpec(memory_space=pltpu.VMEM)
    six = pltpu.VMEM((6, 256, 128), BF16)
    sems = pltpu.SemaphoreType.DMA
    act, kg, bias = pl.pallas_call(
        kernel,
        name="backward",
        out_shape=(
            jax.ShapeDtypeStruct(flat, BF16),
            jax.ShapeDtypeStruct((RUN, CHUNK, channels), BF16),
            jax.ShapeDtypeStruct((8, channels), F32),
        ),
        in_specs=[vmem] * 4,
        out_specs=(vmem,) * 3,
        scratch_shapes=[
            six, six, six, six,
            pltpu.VMEM((6, 256, 384), BF16),
            pltpu.VMEM((6, 272, 384), BF16),
            pltpu.VMEM((9, 384, 128), BF16),
            pltpu.VMEM((128, 512), BF16),
            pltpu.VMEM((RUN, PART, 128), BF16),
            pltpu.VMEM((RUN, PART, 128), BF16),
            pltpu.VMEM((GROUPS, PART, 128), BF16),
            pltpu.VMEM((RUN, CHUNK, 128), BF16),
            sems((2,)), sems((2,)), sems((3,)), sems((4,)), sems, sems((2,)),
            sems((8,)), sems((8,)), sems((8,)), sems((8,)), sems((8,)), sems((8,)),
        ],
        compiler_params=pltpu.CompilerParams(
            collective_id=0, has_side_effects=True, vmem_limit_bytes=40 << 20
        ),
    )(
        saved_in[0].reshape(flat), saved_out[0].reshape(flat), weights[0], cotangent.reshape(flat)
    )
    kernel_sum = kg.reshape(27, channels, channels).astype(F32) * norm_factor
    bias_sum = bias[:1] * norm_factor
    return act.reshape((1,) + cotangent.shape), kernel_sum[None], bias_sum


def solution(mesh):
    placed = (
        P("section", "slab", None, None, None),
        P("section", "slab", None, None, None),
        P("section", None, None, None),
        P("slab", None, None, None),
    )
    return jax.shard_map(
        local,
        mesh=mesh,
        in_specs=placed,
        out_specs=(
            P("section", "slab", None, None, None),
            P("section", None, None, None),
            P("section", None),
        ),
        check_vma=False,
    )
```

time: 1030 us -> 146 us (0.14)
  the two profiles are of different devices: /device:TPU:8 before, /device:TPU:1 now
where the time goes in v1:
time: 146 us
  Pallas kernels  139 us (95%)
  local copies, waits for them, and re-layouts  4.53 us (3%)
  other arithmetic  1.85 us (1%)
    pallas_call x1, Pallas kernels, local(): pl.pallas_call(kernel, name='backward', out_shape=(jax.ShapeDtypeStruct(f...  139 us
    unnamed x9, local copies, waits for them, and re-layouts  4.53 us

profile of v1, /device:TPU:1, one launch (start us, length us, event | category | flops | bytes accessed | tf_op | source)
XLA Modules:
  0.0 146.2 jit_solution(9870553819037313103)
XLA Ops:
  0.6 0.0 copy-start
  0.6 1.2 copy-done
  1.8 0.0 copy-start.1
  1.8 0.9 copy-done.1
  2.7 0.0 copy-start.2
  2.7 0.9 copy-done.2
  3.6 0.0 copy-start.3
  3.6 0.9 copy-done.3
  4.5 139.2 %backward.1 = (bf16[2,256,128]{2,1,0:T(8,128)(2,1)S(1)}, bf16[8,432,128]{2,1,0:T(8,128)(2,1)S(1)}, f32[8,128]{1,0:T(8,128)S(1)}) custom-call(bf16[2,256,128]{2,1,0:T(8,128)(2,1)S(1)} %bitcast.7, bf16[2,256,128]{2,1,0:T(8,128)(2,1)S(1)} %bitcast.8, bf16[27,128,128]{2,1,0:T(8,128)(2,1)S(1)} %bitcast.6, bf16[2,256,128]{2,1,0:T(8,128)(2,1)S(1)} %bitcast.9), custom_call_target="tpu_custom_call" | custom-call | tf_op jit(solution)/shard_map/backward/pallas_call | solution.py:438
  143.7 0.5 slice_multiply_fusion
  144.2 1.3 convert_multiply_fusion
  145.5 0.7 copy.8
Async XLA Ops:
  0.6 1.2 copy-start
  1.8 0.9 copy-start.1
  2.7 0.9 copy-start.2
  3.6 0.9 copy-start.3

commit v2 on v1

v2 whole, which is shorter than its diff:
```python
import math

import jax
import jax.numpy as jnp
from jax import lax
from jax.experimental import pallas as pl
from jax.experimental.pallas import tpu as pltpu
from jax.sharding import PartitionSpec as P

MESH = pl.DeviceIdType.MESH
F32 = jnp.float32
BF16 = jnp.bfloat16

RUN = 8
GROUPS = 8
SHARE = 16
PIECES = 7
AHEAD = 1


def kernel(
    si_ref, so_ref, w_ref, cot_ref,
    act_ref, kg_ref, bias_ref,
    wv, sov, cotv, inc, so6, act6, skip6, s9, w9, mt, mrun, lhs, srun, kgc, rsb, a1, a2,
    load, halo_send, halo_recv, inc_send, inc_recv, skip_send, skip_recv, go,
    si_send, si_recv, edge_send, edge_recv, relay_send, relay_recv,
    mx_send, mx_recv, rs_send, rs_recv,
    a1_send, a1_recv, b1_send, b1_recv, a2_send, a2_recv, b2_send, b2_recv,
):
    sec = lax.axis_index("section")
    j = lax.axis_index("slab")
    n_sec = lax.axis_size("section")
    n_slab = lax.axis_size("slab")
    y = lax.rem(j, RUN)
    g = lax.div(j, RUN)
    odd = lax.rem(sec, 2) == 1
    even = lax.rem(sec, 2) == 0
    has_low = j > 0
    has_high = j < n_slab - 1
    top = sec == n_sec - 1
    first = y == 0
    last = y == RUN - 1
    owner = g < PIECES

    def both(*conditions):
        out = conditions[0]
        for c in conditions[1:]:
            out = jnp.logical_and(out, c)
        return out

    def when(*conditions):
        return pl.when(both(*conditions))

    def loads():
        return (
            pltpu.make_async_copy(so_ref, sov, load.at[0]),
            pltpu.make_async_copy(cot_ref, cotv, load.at[1]),
            pltpu.make_async_copy(w_ref, wv, load.at[2]),
            pltpu.make_async_copy(si_ref, srun.at[pl.ds(1 + 2 * y, 2)], load.at[3]),
        )

    for c in loads():
        c.start()

    barrier = pltpu.get_barrier_semaphore()

    def signal(s, t):
        pl.semaphore_signal(barrier, inc=1, device_id=(s, t), device_id_type=MESH)

    @when(has_low, first)
    def _():
        signal(sec, j - 1)

    @when(has_high, last)
    def _():
        signal(sec, j + 1)

    for d in range(1, RUN):
        signal(sec, g * RUN + lax.rem(y + d, RUN))
    for d in range(1, GROUPS):
        signal(sec, lax.rem(g + d, GROUPS) * RUN + y)

    @when(sec > 0)
    def _():
        signal(sec - 1, j)

    @when(jnp.logical_not(top))
    def _():
        signal(sec + 1, j)

    @when(even, sec > 0, has_low)
    def _():
        signal(sec - 1, j - 1)

    @when(even, sec > 0, has_high)
    def _():
        signal(sec - 1, j + 1)

    @when(odd, jnp.logical_not(top), has_low)
    def _():
        signal(sec + 1, j - 1)

    @when(odd, jnp.logical_not(top), has_high)
    def _():
        signal(sec + 1, j + 1)

    @when(sec >= 4)
    def _():
        signal(sec - 4, j)

    @when(sec < 4)
    def _():
        signal(sec + 4, j)

    def one(*conditions):
        return jnp.where(both(*conditions), 1, 0)

    diagonal = jnp.logical_or(both(even, sec > 0), both(odd, jnp.logical_not(top)))
    expected = (
        RUN - 1 + GROUPS - 1 + 1
        + one(has_low, first) + one(has_high, last)
        + one(sec > 0) + one(jnp.logical_not(top))
        + one(diagonal, has_low) + one(diagonal, has_high)
    )

    blank = jnp.zeros((2, 256, 128), BF16)

    @when(jnp.logical_not(has_low))
    def _():
        so6[0:2] = blank

        @when(odd)
        def _():
            inc[0:2] = blank

    @when(jnp.logical_not(has_high))
    def _():
        so6[4:6] = blank

        @when(odd)
        def _():
            inc[4:6] = blank

    @when(g == 0)
    def _():
        srun[0] = blank[0]

    @when(g == GROUPS - 1)
    def _():
        srun[2 * RUN + 1] = blank[0]

    load_so, load_cot, load_w, load_si = loads()
    load_so.wait()
    load_cot.wait()

    @when(top)
    def _():
        so6[2:4] = jnp.where(sov[...].astype(F32) > 0, cotv[...].astype(F32), 0.0).astype(BF16)

    @when(jnp.logical_not(top))
    def _():
        so6[2:4] = sov[...]

    load_w.wait()

    def turn(k, carry):
        dy, dx, dz = lax.div(k, 9), lax.rem(lax.div(k, 3), 3), lax.rem(k, 3)
        tile = wv[k].astype(F32).T.astype(BF16)
        rows = pl.ds(pl.multiple_of(dx * 384 + dz * 128, 128), 128)
        w9[rows, pl.ds(pl.multiple_of(dy * 128, 128), 128)] = tile
        return carry

    lax.fori_loop(0, 27, turn, 0)
    load_si.wait()

    pl.semaphore_wait(barrier, expected)

    def remote(src, dst, ss, rs, s, t):
        return pltpu.make_async_remote_copy(
            src_ref=src, dst_ref=dst, send_sem=ss, recv_sem=rs,
            device_id=(s, t), device_id_type=MESH,
        )

    def halo(low):
        own = so6.at[2:4]
        if low:
            return remote(own, so6.at[4:6], halo_send.at[0], halo_recv.at[0], sec, j - 1)
        return remote(own, so6.at[0:2], halo_send.at[1], halo_recv.at[1], sec, j + 1)

    @when(has_low)
    def _():
        halo(True).start()

    @when(has_high)
    def _():
        halo(False).start()

    def mate(d):
        return lax.rem(y + d, RUN)

    def mate_in(d):
        return lax.rem(y + RUN - d, RUN)

    def peer(d):
        return lax.rem(g + d, GROUPS)

    def peer_in(d):
        return lax.rem(g + GROUPS - d, GROUPS)

    def si_out(d):
        own = srun.at[pl.ds(1 + 2 * y, 2)]
        return remote(own, own, si_send.at[d], si_recv.at[d], sec, g * RUN + mate(d))

    def si_in(d):
        rows = srun.at[pl.ds(1 + 2 * mate_in(d), 2)]
        return remote(rows, rows, si_send.at[d], si_recv.at[d], sec, g * RUN + mate_in(d))

    def edge(low):
        if low:
            return remote(srun.at[1], srun.at[2 * RUN + 1], edge_send.at[0], edge_recv.at[0], sec, j - 1)
        return remote(srun.at[2 * RUN], srun.at[0], edge_send.at[1], edge_recv.at[1], sec, j + 1)

    def relay(low, d):
        row = srun.at[0] if low else srun.at[2 * RUN + 1]
        i = 0 if low else 1
        return remote(row, row, relay_send.at[i, d], relay_recv.at[i], sec, g * RUN + mate(d))

    low_row = g > 0
    high_row = g < GROUPS - 1

    def gather_run():
        @when(first, low_row)
        def _():
            edge(True).start()

        @when(last, high_row)
        def _():
            edge(False).start()

        for d in range(1, RUN):
            si_out(d).start()

        @when(first, low_row)
        def _():
            edge(False).wait_recv()
            for d in range(1, RUN):
                relay(True, d).start()

        @when(last, high_row)
        def _():
            edge(True).wait_recv()
            for d in range(1, RUN):
                relay(False, d).start()

    @when(has_low)
    def _():
        halo(False).wait_recv()

    @when(has_high)
    def _():
        halo(True).wait_recv()

    early = sec < n_sec - 2
    late = sec >= n_sec - 2

    @when(early)
    def _():
        gather_run()

    def to_inc(which):
        own = act6.at[2:4]
        if which == 0:
            return remote(own, inc.at[2:4], inc_send.at[0], inc_recv.at[0], sec - 1, j)
        if which == 1:
            return remote(own, inc.at[4:6], inc_send.at[1], inc_recv.at[1], sec - 1, j - 1)
        if which == 2:
            return remote(own, inc.at[0:2], inc_send.at[2], inc_recv.at[2], sec - 1, j + 1)
        return remote(act6.at[1:5], inc.at[1:5], inc_send.at[0], inc_recv.at[3], sec - 1, j)

    def to_skip(rows):
        if rows == 4:
            return remote(act6.at[1:5], skip6.at[1:5], skip_send, skip_recv.at[0], sec - 4, j)
        return remote(act6.at[2:4], skip6.at[2:4], skip_send, skip_recv.at[1], sec - 4, j)

    @when(odd, jnp.logical_not(top))
    def _():
        to_inc(0).wait_recv()

        @when(has_high)
        def _():
            to_inc(1).wait_recv()

        @when(has_low)
        def _():
            to_inc(2).wait_recv()

    @when(even)
    def _():
        to_inc(3).wait_recv()

    depth = lax.broadcasted_iota(jnp.int32, (32, 8, 128), 1)
    edge_x = jnp.zeros((8, 128), F32)

    def stack_row(r, carry):
        held = so6[r].astype(F32)
        arrived = jnp.where(held > 0, inc[r].astype(F32), 0.0)
        m = jnp.where(top, held, arrived).reshape(32, 8, 128)
        up = jnp.where(depth == 7, 0.0, pltpu.roll(m, 7, 1)).reshape(256, 128)
        down = jnp.where(depth == 0, 0.0, pltpu.roll(m, 1, 1)).reshape(256, 128)
        for b, v in enumerate((up, m.reshape(256, 128), down)):
            at = b * 128
            s9[r, :, at:at + 128] = jnp.concatenate([v[8:], edge_x], 0).astype(BF16)
            s9[r, :, at + 384:at + 512] = v.astype(BF16)
            s9[r, :, at + 768:at + 896] = jnp.concatenate([edge_x, v[:-8]], 0).astype(BF16)
        return carry

    @when(odd)
    def _():
        lax.fori_loop(0, 6, stack_row, 0)

    @when(even)
    def _():
        lax.fori_loop(1, 5, stack_row, 0)

    def conv_rows(lo, hi):
        sums = {}
        for t in range(lo - 1, hi + 1):
            reach = [dy for dy in (-1, 0, 1) if lo <= t + dy < hi]
            p = jnp.dot(
                s9[t], w9[:, (reach[0] + 1) * 128:(reach[-1] + 2) * 128],
                preferred_element_type=F32,
            )
            for i, dy in enumerate(reach):
                v = p[:, i * 128:(i + 1) * 128]
                sums[t + dy] = v if dy == 1 or t + dy not in sums else sums[t + dy] + v
            r = t - 1
            if lo <= r < hi:
                act6[r] = jnp.where(sec < 4, sums[r] + skip6[r].astype(F32), sums[r]).astype(BF16)

    def conv():
        @when(sec < 4, odd)
        def _():
            to_skip(4).wait_recv()

        @when(sec < 4, even)
        def _():
            to_skip(2).wait_recv()

        @when(odd)
        def _():
            conv_rows(1, 5)

        @when(even)
        def _():
            conv_rows(2, 4)

    @when(sec > 0)
    def _():
        conv()

        @when(odd)
        def _():
            to_inc(3).start()

        @when(even)
        def _():
            to_inc(0).start()

            @when(has_low)
            def _():
                to_inc(1).start()

            @when(has_high)
            def _():
                to_inc(2).start()

    for r in range(2):
        for h in range(2):
            block = s9[2 + r, h * 128:(h + 1) * 128, 512:640].astype(F32).T.astype(BF16)
            at = r * 256 + h * 128
            mt[:, :, at:at + 128] = block.reshape(RUN, SHARE, 128)

    @when(even, sec > 0)
    def _():
        to_inc(0).wait_send()

        @when(has_low)
        def _():
            to_inc(1).wait_send()

        @when(has_high)
        def _():
            to_inc(2).wait_send()

        pl.semaphore_signal(go, inc=1, device_id=(sec + 1, j), device_id_type=MESH)

    @when(odd, sec > 1)
    def _():
        pl.semaphore_wait(go, 1)

    @when(sec >= 4, odd)
    def _():
        to_skip(4).start()

    @when(sec >= 4, even)
    def _():
        to_skip(2).start()

    def mx_out(d):
        return remote(mt.at[mate(d)], mrun.at[y], mx_send.at[d], mx_recv.at[d], sec, g * RUN + mate(d))

    def mx_in(d):
        return remote(mt.at[y], mrun.at[mate_in(d)], mx_send.at[d], mx_recv.at[d], sec, g * RUN + mate_in(d))

    for d in range(1, RUN):
        mx_out(d).start()
    mrun[y] = mt[y]

    @when(sec == 0)
    def _():
        conv()

    @when(late)
    def _():
        gather_run()

    lane = lax.broadcasted_iota(jnp.int32, (SHARE, 512), 1)
    cell_x = lax.rem(lax.div(lane, 8), 32)
    cell_z = lax.rem(lane, 8)
    fits = []
    for dx in (-1, 0, 1):
        for dz in (-1, 0, 1):
            fits.append(both(cell_x - dx >= 0, cell_x - dx < 32, cell_z - dz >= 0, cell_z - dz < 8))

    for d in range(1, RUN):
        mx_in(d).wait_recv()

    bias = jnp.zeros((SHARE, 512), F32)
    for u in range(RUN):
        m = mrun[u].astype(F32)
        bias = bias + m
        for i, ok in enumerate(fits):
            step = ((i // 3 - 1) * 8 + i % 3 - 1) % 512
            moved = m if step == 0 else jnp.where(ok, pltpu.roll(m, step, 1), 0.0)
            lhs[i * SHARE:(i + 1) * SHARE, u * 512:(u + 1) * 512] = moved.astype(BF16)

    for d in range(1, RUN):
        si_in(d).wait_recv()

    @when(low_row, jnp.logical_not(first))
    def _():
        relay(True, 1).wait_recv()

    @when(high_row, jnp.logical_not(last))
    def _():
        relay(False, 1).wait_recv()

    column = lax.broadcasted_iota(jnp.int32, (SHARE, 128), 1)

    def split(total):
        head = total.astype(BF16).astype(F32)
        return jnp.where(column == 0, head, jnp.where(column == 1, total - head, 0.0))

    for dy in range(3):
        block = jnp.dot(
            lhs[...], srun[dy:dy + 2 * RUN].reshape(RUN * 512, 128), preferred_element_type=F32
        ).astype(BF16)
        for i in range(9):
            t = dy * 9 + i
            kgc[t // 4, t % 4] = block[i * SHARE:(i + 1) * SHARE]
    kgc[6, 3] = split(jnp.sum(bias, axis=1, keepdims=True)).astype(BF16)

    def rs_out(d):
        return remote(
            kgc.at[peer(d)], rsb.at[d], rs_send.at[d], rs_recv.at[d], sec, peer(d) * RUN + y
        )

    def rs_in(d):
        return remote(
            kgc.at[0], rsb.at[d], rs_send.at[d], rs_recv.at[d], sec, peer_in(d) * RUN + y
        )

    for d in range(1, GROUPS):
        @when(peer(d) < PIECES)
        def _():
            rs_out(d).start()

    def a1_out(d):
        part = a1.at[y, g]
        return remote(part, part, a1_send.at[d], a1_recv.at[d], sec, peer(d) * RUN + y)

    def a1_in(d):
        part = a1.at[y, peer_in(d)]
        return remote(part, part, a1_send.at[d], a1_recv.at[d], sec, peer_in(d) * RUN + y)

    def b1_out(d):
        return remote(a1.at[y], a1.at[y], b1_send.at[d], b1_recv.at[d], sec, g * RUN + mate(d))

    def b1_in(d):
        part = a1.at[mate_in(d)]
        return remote(part, part, b1_send.at[d], b1_recv.at[d], sec, g * RUN + mate_in(d))

    def a2_out(d):
        part = a2.at[g, y]
        return remote(part, part, a2_send.at[d], a2_recv.at[d], sec, g * RUN + mate(d))

    def a2_in(d):
        part = a2.at[g, mate_in(d)]
        return remote(part, part, a2_send.at[d], a2_recv.at[d], sec, g * RUN + mate_in(d))

    def b2_out(d):
        return remote(a2.at[g], a2.at[g], b2_send.at[d], b2_recv.at[d], sec, peer(d) * RUN + y)

    def b2_in(d):
        part = a2.at[peer_in(d)]
        return remote(part, part, b2_send.at[d], b2_recv.at[d], sec, peer_in(d) * RUN + y)

    @when(owner)
    def _():
        for d in range(1, GROUPS):
            rs_in(d).wait_recv()
        total = kgc[g].astype(F32)
        for d in range(1, GROUPS):
            total = total + rsb[d].astype(F32)
        pair = split(total[3, :, 0:1] + total[3, :, 1:2])
        final = jnp.where(g == PIECES - 1, pair, total[3])
        a1[y, g] = total[:AHEAD].astype(BF16)
        a2[g, y, 0:3 - AHEAD] = total[AHEAD:3].astype(BF16)
        a2[g, y, 3 - AHEAD] = final.astype(BF16)
        for d in range(1, GROUPS):
            a1_out(d).start()
        for d in range(1, RUN):
            a2_out(d).start()

    act_ref[...] = act6[2:4]

    @when(owner)
    def _():
        for d in range(1, RUN):
            a2_in(d).wait_recv()
        for d in range(1, GROUPS):
            b2_out(d).start()

    for d in range(1, GROUPS):
        @when(peer_in(d) < PIECES)
        def _():
            a1_in(d).wait_recv()
    for d in range(1, RUN):
        b1_out(d).start()

    @when(has_low)
    def _():
        halo(True).wait_send()

    @when(has_high)
    def _():
        halo(False).wait_send()

    @when(first, low_row)
    def _():
        edge(True).wait_send()
        for d in range(1, RUN):
            relay(True, d).wait_send()

    @when(last, high_row)
    def _():
        edge(False).wait_send()
        for d in range(1, RUN):
            relay(False, d).wait_send()

    @when(sec > 0, odd)
    def _():
        to_inc(3).wait_send()

    @when(sec >= 4, odd)
    def _():
        to_skip(4).wait_send()

    @when(sec >= 4, even)
    def _():
        to_skip(2).wait_send()

    for d in range(1, RUN):
        si_out(d).wait_send()
        mx_out(d).wait_send()

        @when(peer(d) < PIECES)
        def _():
            rs_out(d).wait_send()

    @when(owner)
    def _():
        for d in range(1, RUN):
            a1_out(d).wait_send()
            a2_out(d).wait_send()
            b2_out(d).wait_send()

    for d in range(1, RUN):
        b1_out(d).wait_send()
    for d in range(1, RUN):
        b1_in(d).wait_recv()
    for d in range(1, GROUPS):
        @when(peer_in(d) < PIECES)
        def _():
            b2_in(d).wait_recv()

    for t in range(28):
        q, i = t // 4, t % 4
        if i < AHEAD:
            tile = a1[:, q, i]
        else:
            tile = a2[q, :, i - AHEAD]
        tile = tile.reshape(128, 128).astype(F32).T
        if t < 27:
            kg_ref[t] = tile.astype(BF16)
        else:
            bias_ref[...] = jnp.broadcast_to(tile[0:1] + tile[1:2], (8, 128))


def local(saved_in, saved_out, weights, cotangent):
    rows_y, cells_x, cells_z, channels = cotangent.shape
    norm_factor = 1.0 / math.sqrt(rows_y * lax.axis_size("slab") * cells_x * cells_z)
    flat = (rows_y, cells_x * cells_z, channels)
    vmem = pl.BlockSpec(memory_space=pltpu.VMEM)
    hbm = pl.BlockSpec(memory_space=pl.ANY)
    six = pltpu.VMEM((6, 256, 128), BF16)
    two = pltpu.VMEM((2, 256, 128), BF16)
    sems = pltpu.SemaphoreType.DMA
    act, kg, bias = pl.pallas_call(
        kernel,
        name="backward",
        out_shape=(
            jax.ShapeDtypeStruct(flat, BF16),
            jax.ShapeDtypeStruct((27, channels, channels), BF16),
            jax.ShapeDtypeStruct((8, channels), F32),
        ),
        in_specs=[hbm] * 4,
        out_specs=(vmem,) * 3,
        scratch_shapes=[
            pltpu.VMEM((27, 128, 128), BF16), two, two,
            six, six, six, six,
            pltpu.VMEM((6, 256, 1152), BF16),
            pltpu.VMEM((1152, 384), BF16),
            pltpu.VMEM((RUN, SHARE, 512), BF16),
            pltpu.VMEM((RUN, SHARE, 512), BF16),
            pltpu.VMEM((9 * SHARE, RUN * 512), BF16),
            pltpu.VMEM((2 * RUN + 2, 256, 128), BF16),
            pltpu.VMEM((PIECES, 4, SHARE, 128), BF16),
            pltpu.VMEM((GROUPS, 4, SHARE, 128), BF16),
            pltpu.VMEM((RUN, PIECES, AHEAD, SHARE, 128), BF16),
            pltpu.VMEM((PIECES, RUN, 4 - AHEAD, SHARE, 128), BF16),
            sems((4,)), sems((2,)), sems((2,)), sems((3,)), sems((4,)), sems, sems((2,)),
            pltpu.SemaphoreType.REGULAR,
            sems((8,)), sems((8,)), sems((2,)), sems((2,)), sems((2, 8)), sems((2,)),
            sems((8,)), sems((8,)), sems((8,)), sems((8,)),
            sems((8,)), sems((8,)), sems((8,)), sems((8,)),
            sems((8,)), sems((8,)), sems((8,)), sems((8,)),
        ],
        compiler_params=pltpu.CompilerParams(
            collective_id=0, has_side_effects=True, vmem_limit_bytes=56 << 20
        ),
    )(
        saved_in[0].reshape(flat), saved_out[0].reshape(flat), weights[0], cotangent.reshape(flat)
    )
    kernel_sum = kg.astype(F32) * norm_factor
    bias_sum = bias[:1] * norm_factor
    return act.reshape((1,) + cotangent.shape), kernel_sum[None], bias_sum


def solution(mesh):
    placed = (
        P("section", "slab", None, None, None),
        P("section", "slab", None, None, None),
        P("section", None, None, None),
        P("slab", None, None, None),
    )
    return jax.shard_map(
        local,
        mesh=mesh,
        in_specs=placed,
        out_specs=(
            P("section", "slab", None, None, None),
            P("section", None, None, None),
            P("section", None),
        ),
        check_vma=False,
    )
```

time: 146 us -> 113 us (0.77)
  the two profiles are of different devices: /device:TPU:1 before, /device:TPU:8 now
where the time goes in v2:
time: 113 us
  Pallas kernels  108 us (96%)
  other arithmetic  3.81 us (3%)
    pallas_call x1, Pallas kernels, local(): pl.pallas_call(kernel, name='backward', out_shape=(jax.ShapeDtypeStruct(f...  108 us
    broadcast_in_dim x1, other arithmetic, local(): return (act.reshape((1,) + cotangent.shape), kernel_sum[None], bias_sum)  2.58 us

profile of v2, /device:TPU:8, one launch (start us, length us, event | category | flops | bytes accessed | tf_op | source)
XLA Modules:
  0.0 113.0 jit_solution(17417201511181148392)
XLA Ops:
  0.6 107.9 %backward.1 = (bf16[2,256,128]{2,1,0:T(8,128)(2,1)}, bf16[27,128,128]{2,1,0:T(8,128)(2,1)}, f32[8,128]{1,0:T(8,128)}) custom-call(bf16[2,256,128]{2,1,0:T(8,128)(2,1)} %bitcast.8, bf16[2,256,128]{2,1,0:T(8,128)(2,1)} %bitcast.9, bf16[27,128,128]{2,1,0:T(8,128)(2,1)} %bitcast.7, bf16[2,256,128]{2,1,0:T(8,128)(2,1)} %bitcast.10), custom_call_target="tpu_custom_call" | custom-call | tf_op jit(solution)/shard_map/backward/pallas_call | solution.py:629
  108.5 0.0 copy-start
  108.5 1.2 %slice_multiply_fusion = f32[1,128]{1,0:T(1,128)} fusion(f32[8,128]{1,0:T(8,128)} %get-tuple-element.8), kind=kLoop, calls=%fused_computation.1 | loop fusion | flops 128 | bytes 1024 | tf_op jit(solution)/shard_map/mul | solution.py:666
  109.8 2.6 %multiply_bitcast_fusion = f32[1,27,128,128]{3,2,1,0:T(8,128)} fusion(bf16[27,128,128]{2,1,0:T(8,128)(2,1)} %get-tuple-element.7), kind=kLoop, calls=%fused_computation | loop fusion | flops 884736 | bytes 2654208 | tf_op jit(solution)/shard_map/broadcast_in_dim | solution.py:667
  112.4 0.0 copy-done
  112.4 0.7 copy.8
Async XLA Ops:
  108.5 3.8 %copy-start = (bf16[2,256,128]{2,1,0:T(8,128)(2,1)S(1)}, bf16[2,256,128]{2,1,0:T(8,128)(2,1)}, u32[]{:S(2)}) copy-start(bf16[2,256,128]{2,1,0:T(8,128)(2,1)} %get-tuple-element.6) | copy-start | bytes 393220

commit v3 on v2

v3 whole, which is shorter than its diff:
```python
import functools
import math

import jax
import jax.numpy as jnp
from jax import lax
from jax.experimental import pallas as pl
from jax.experimental.pallas import tpu as pltpu
from jax.sharding import PartitionSpec as P

MESH = pl.DeviceIdType.MESH
F32 = jnp.float32
BF16 = jnp.bfloat16

RUN = 8
GROUPS = 8
SHARE = 16
WIDE = 4
TILES = 7
AHEAD = 2


def kernel(
    si_ref, so_ref, w_ref, cot_ref,
    act_ref, a1, a2,
    wv, sov, cotv, inc, so6, act6, skip6, s9, w9, mt, mtx, mrun, ends, lhs, srun, kgc, rsb,
    load, halo_send, halo_recv, row_send, row_recv, slab_send, slab_recv, skip_send, skip_recv, go,
    up_send, up_recv, down_send, down_recv, end_send, end_recv,
    mx_send, mx_recv, rs_send, rs_recv,
    a1_send, a1_recv, b1_send, b1_recv, a2_send, a2_recv, b2_send, b2_recv,
):
    sec = lax.axis_index("section")
    j = lax.axis_index("slab")
    n_sec = lax.axis_size("section")
    n_slab = lax.axis_size("slab")
    y = lax.rem(j, RUN)
    g = lax.div(j, RUN)
    odd = lax.rem(sec, 2) == 1
    even = lax.rem(sec, 2) == 0
    has_low = j > 0
    has_high = j < n_slab - 1
    top = sec == n_sec - 1
    first = y == 0
    last = y == RUN - 1
    x = lax.div(g, 2)
    high = lax.rem(g, 2)

    def both(*conditions):
        out = conditions[0]
        for c in conditions[1:]:
            out = jnp.logical_and(out, c)
        return out

    def when(*conditions):
        return pl.when(both(*conditions))

    def loads():
        return (
            pltpu.make_async_copy(so_ref, sov, load.at[0]),
            pltpu.make_async_copy(cot_ref, cotv, load.at[1]),
            pltpu.make_async_copy(w_ref, wv, load.at[2]),
            pltpu.make_async_copy(si_ref, srun.at[pl.ds(2 * y, 2)], load.at[3]),
        )

    for c in loads():
        c.start()

    barrier = pltpu.get_barrier_semaphore()

    def signal(s, t):
        pl.semaphore_signal(barrier, inc=1, device_id=(s, t), device_id_type=MESH)

    @when(has_low, first)
    def _():
        signal(sec, j - 1)

    @when(has_high, last)
    def _():
        signal(sec, j + 1)

    for d in range(1, RUN):
        signal(sec, g * RUN + lax.rem(y + d, RUN))
    for d in range(1, GROUPS):
        signal(sec, lax.rem(g + d, GROUPS) * RUN + y)

    @when(sec > 0)
    def _():
        signal(sec - 1, j)

    @when(jnp.logical_not(top))
    def _():
        signal(sec + 1, j)

    @when(even, sec > 0, has_low)
    def _():
        signal(sec - 1, j - 1)

    @when(even, sec > 0, has_high)
    def _():
        signal(sec - 1, j + 1)

    @when(odd, jnp.logical_not(top), has_low)
    def _():
        signal(sec + 1, j - 1)

    @when(odd, jnp.logical_not(top), has_high)
    def _():
        signal(sec + 1, j + 1)

    @when(sec >= 4)
    def _():
        signal(sec - 4, j)

    @when(sec < 4)
    def _():
        signal(sec + 4, j)

    def one(*conditions):
        return jnp.where(both(*conditions), 1, 0)

    diagonal = jnp.logical_or(both(even, sec > 0), both(odd, jnp.logical_not(top)))
    expected = (
        RUN - 1 + GROUPS - 1 + 1
        + one(has_low, first) + one(has_high, last)
        + one(sec > 0) + one(jnp.logical_not(top))
        + one(diagonal, has_low) + one(diagonal, has_high)
    )

    blank = jnp.zeros((2, 256, 128), BF16)

    @when(jnp.logical_not(has_low))
    def _():
        so6[0:2] = blank

        @when(odd)
        def _():
            inc[0:2] = blank

    @when(jnp.logical_not(has_high))
    def _():
        so6[4:6] = blank

        @when(odd)
        def _():
            inc[4:6] = blank

    @when(g == 0)
    def _():
        ends[0] = jnp.zeros((SHARE, 256), BF16)

    @when(g == GROUPS - 1)
    def _():
        ends[1] = jnp.zeros((SHARE, 256), BF16)

    load_so, load_cot, load_w, load_si = loads()
    load_so.wait()
    load_cot.wait()

    @when(top)
    def _():
        so6[2:4] = jnp.where(sov[...].astype(F32) > 0, cotv[...].astype(F32), 0.0).astype(BF16)

    @when(jnp.logical_not(top))
    def _():
        so6[2:4] = sov[...]

    load_w.wait()

    def turn(k, carry):
        dy, dx, dz = lax.div(k, 9), lax.rem(lax.div(k, 3), 3), lax.rem(k, 3)
        tile = wv[k].astype(F32).T.astype(BF16)
        rows = pl.ds(pl.multiple_of(dx * 384 + dz * 128, 128), 128)
        w9[rows, pl.ds(pl.multiple_of(dy * 128, 128), 128)] = tile
        return carry

    lax.fori_loop(0, 27, turn, 0)
    load_si.wait()

    pl.semaphore_wait(barrier, expected)

    def remote(src, dst, ss, rs, s, t):
        return pltpu.make_async_remote_copy(
            src_ref=src, dst_ref=dst, send_sem=ss, recv_sem=rs,
            device_id=(s, t), device_id_type=MESH,
        )

    def halo(low):
        own = so6.at[2:4]
        if low:
            return remote(own, so6.at[4:6], halo_send.at[0], halo_recv.at[0], sec, j - 1)
        return remote(own, so6.at[0:2], halo_send.at[1], halo_recv.at[1], sec, j + 1)

    @when(has_low)
    def _():
        halo(True).start()

    @when(has_high)
    def _():
        halo(False).start()

    def mate(d):
        return lax.rem(y + d, RUN)

    def mate_in(d):
        return lax.rem(y + RUN - d, RUN)

    def peer(d):
        return lax.rem(g + d, GROUPS)

    def peer_in(d):
        return lax.rem(g + GROUPS - d, GROUPS)

    def rows_of(origin):
        return srun.at[pl.ds(2 * origin, 2)]

    def up_out(step):
        rows = rows_of(lax.rem(y + RUN - step, RUN))
        return remote(rows, rows, up_send.at[step], up_recv.at[step], sec, g * RUN + mate(1))

    def up_in(step):
        rows = rows_of(lax.rem(y + RUN - step - 1, RUN))
        return remote(rows, rows, up_send.at[step], up_recv.at[step], sec, g * RUN + mate(1))

    def down_out(step):
        rows = rows_of(lax.rem(y + step, RUN))
        return remote(rows, rows, down_send.at[step], down_recv.at[step], sec, g * RUN + mate(RUN - 1))

    def down_in(step):
        rows = rows_of(lax.rem(y + step + 1, RUN))
        return remote(rows, rows, down_send.at[step], down_recv.at[step], sec, g * RUN + mate(RUN - 1))

    low_row = g > 0
    high_row = g < GROUPS - 1

    def gather_run():
        for step in range(4):
            up_out(step).start()
            if step < 3:
                down_out(step).start()
            up_in(step).wait_recv()
            if step < 3:
                down_in(step).wait_recv()

    def halo_wait(low):
        if low:
            @when(has_low)
            def _():
                halo(False).wait_recv()
        else:
            @when(has_high)
            def _():
                halo(True).wait_recv()

    early = sec < n_sec - 2
    late = sec >= n_sec - 2

    @when(early)
    def _():
        gather_run()

    def to_sibling(r):
        return remote(act6.at[r], inc.at[r], row_send.at[r - 1], row_recv.at[r - 1], sec - 1, j)

    def to_slab(i, which):
        at = (2, 4, 0)[which] + i
        k = 3 * i + which
        return remote(
            act6.at[2 + i], inc.at[at], slab_send.at[k], slab_recv.at[k], sec - 1, j + (0, -1, 1)[which]
        )

    def slab_sends(i, act):
        getattr(to_slab(i, 0), act)()

        @when(has_low)
        def _():
            getattr(to_slab(i, 1), act)()

        @when(has_high)
        def _():
            getattr(to_slab(i, 2), act)()

    def to_skip(rows):
        if rows == 4:
            return remote(act6.at[1:5], skip6.at[1:5], skip_send, skip_recv.at[0], sec - 4, j)
        return remote(act6.at[2:4], skip6.at[2:4], skip_send, skip_recv.at[1], sec - 4, j)

    depth = lax.broadcasted_iota(jnp.int32, (32, 8, 128), 1)
    edge_x = jnp.zeros((8, 128), F32)

    def stack_row(r, carry):
        held = so6[r].astype(F32)
        arrived = jnp.where(held > 0, inc[r].astype(F32), 0.0)
        m = jnp.where(top, held, arrived).reshape(32, 8, 128)
        up = jnp.where(depth == 7, 0.0, pltpu.roll(m, 7, 1)).reshape(256, 128)
        down = jnp.where(depth == 0, 0.0, pltpu.roll(m, 1, 1)).reshape(256, 128)
        for b, v in enumerate((up, m.reshape(256, 128), down)):
            at = b * 128
            s9[r, :, at:at + 128] = jnp.concatenate([v[8:], edge_x], 0).astype(BF16)
            s9[r, :, at + 384:at + 512] = v.astype(BF16)
            s9[r, :, at + 768:at + 896] = jnp.concatenate([edge_x, v[:-8]], 0).astype(BF16)
        return carry

    def layer(lo, hi, steps, done):
        sums, count = {}, {}
        for ready, rows in steps:
            ready()
            for t in rows:
                reach = [dy for dy in (-1, 0, 1) if lo <= t + dy < hi]
                p = jnp.dot(
                    s9[t], w9[:, (reach[0] + 1) * 128:(reach[-1] + 2) * 128],
                    preferred_element_type=F32,
                )
                for i, dy in enumerate(reach):
                    r = t + dy
                    v = p[:, i * 128:(i + 1) * 128]
                    sums[r] = sums[r] + v if r in sums else v
                    count[r] = count.get(r, 0) + 1
                    if count[r] == 3:
                        total = sums.pop(r)
                        total = jnp.where(sec < 4, total + skip6[r].astype(F32), total)
                        act6[r] = total.astype(BF16)
                        done(r)

    def odd_layer(low_first):
        def own():
            @when(jnp.logical_not(top))
            def _():
                to_slab(0, 0).wait_recv()
                to_slab(1, 0).wait_recv()

            lax.fori_loop(2, 4, stack_row, 0)

        def side(low):
            halo_wait(low)

            @when(jnp.logical_not(top), has_low if low else has_high)
            def _():
                for i in range(2):
                    to_slab(i, 2 if low else 1).wait_recv()

            at = 0 if low else 4
            lax.fori_loop(at, at + 2, stack_row, 0)

        @when(sec < 4)
        def _():
            to_skip(4).wait_recv()

        lows = (lambda: side(True), (0, 1))
        highs = (lambda: side(False), (4, 5))
        order = [lows, highs] if low_first else [highs, lows]
        layer(1, 5, [(own, (2, 3))] + order, lambda r: to_sibling(r).start())

    def even_layer(low_first):
        rows = (1, 2, 3, 4) if low_first else (4, 3, 2, 1)

        def ready(r):
            to_sibling(r).wait_recv()
            lax.fori_loop(r, r + 1, stack_row, 0)

        @when(sec < 4)
        def _():
            to_skip(2).wait_recv()

        layer(
            2, 4, [(lambda r=r: ready(r), (r,)) for r in rows],
            lambda r: slab_sends(r - 2, "start"),
        )

    @when(odd, first)
    def _():
        odd_layer(False)

    @when(odd, jnp.logical_not(first))
    def _():
        odd_layer(True)

    @when(even)
    def _():
        halo_wait(True)
        halo_wait(False)

    @when(even, sec > 0, first)
    def _():
        even_layer(False)

    @when(even, sec > 0, jnp.logical_not(first))
    def _():
        even_layer(True)

    @when(sec == 0)
    def _():
        for r in range(1, 5):
            to_sibling(r).wait_recv()
        lax.fori_loop(1, 5, stack_row, 0)

    def turned(r, h):
        block = s9[r, h * 128:(h + 1) * 128, 512:640].astype(F32).T.astype(BF16)
        return block.reshape(RUN, SHARE, 128)

    for r in range(2):
        for h in range(2):
            at = r * 256 + h * 128
            mt[:, :, at:at + 128] = turned(2 + r, h)

    for outer, r in ((both(first, low_row), 1), (both(last, high_row), 4)):
        @when(outer)
        def _():
            for h in range(2):
                mtx[:, :, h * 128:(h + 1) * 128] = turned(r, h)

    @when(even, sec > 0)
    def _():
        slab_sends(0, "wait_send")
        slab_sends(1, "wait_send")
        pl.semaphore_signal(go, inc=1, device_id=(sec + 1, j), device_id_type=MESH)

    @when(odd, sec > 1)
    def _():
        pl.semaphore_wait(go, 1)

    @when(sec >= 4, odd)
    def _():
        to_skip(4).start()

    @when(sec >= 4, even)
    def _():
        to_skip(2).start()

    def mx_out(d):
        return remote(mt.at[mate(d)], mrun.at[y], mx_send.at[d], mx_recv.at[d], sec, g * RUN + mate(d))

    def mx_in(d):
        return remote(mt.at[y], mrun.at[mate_in(d)], mx_send.at[d], mx_recv.at[d], sec, g * RUN + mate_in(d))

    def end_out(i, d):
        return remote(mtx.at[mate(d)], ends.at[i], end_send.at[d], end_recv.at[i], sec, g * RUN + mate(d))

    for d in range(1, RUN):
        mx_out(d).start()
    mrun[y] = mt[y]

    has_end = (both(first, low_row), both(last, high_row))
    for i in range(2):
        @when(has_end[i])
        def _():
            for d in range(1, RUN):
                end_out(i, d).start()
            ends[i] = mtx[y]

    @when(sec == 0)
    def _():
        to_skip(2).wait_recv()
        layer(2, 4, [(lambda: None, (1, 2, 3, 4))], lambda r: None)

    @when(late)
    def _():
        gather_run()

    lane = lax.broadcasted_iota(jnp.int32, (SHARE, 512), 1)
    cell_x = lax.rem(lax.div(lane, 8), 32)
    cell_z = lax.rem(lane, 8)
    fits = []
    for dx in (-1, 0, 1):
        for dz in (-1, 0, 1):
            fits.append(both(cell_x - dx >= 0, cell_x - dx < 32, cell_z - dz >= 0, cell_z - dz < 8))

    for d in range(1, RUN):
        mx_in(d).wait_recv()

    for i, (there, away) in enumerate(((low_row, y > 0), (high_row, y < RUN - 1))):
        @when(there, away)
        def _():
            end_out(i, 1).wait_recv()

    def spread(m, at, width):
        for i, ok in enumerate(fits):
            step = ((i // 3 - 1) * 8 + i % 3 - 1) % width
            moved = m if step == 0 else jnp.where(ok[:, :width], pltpu.roll(m, step, 1), 0.0)
            lhs[i * SHARE:(i + 1) * SHARE, at:at + width] = moved.astype(BF16)

    bias = jnp.zeros((SHARE, 512), F32)
    spread(ends[0].astype(F32), 0, 256)
    for u in range(RUN):
        m = mrun[u].astype(F32)
        bias = bias + m
        spread(m, 256 + u * 512, 512)
    spread(ends[1].astype(F32), 256 + RUN * 512, 256)

    column = lax.broadcasted_iota(jnp.int32, (SHARE, 128), 1)

    def split(total):
        head = total.astype(BF16).astype(F32)
        return jnp.where(column == 0, head, jnp.where(column == 1, total - head, 0.0))

    for dy in range(3):
        block = jnp.dot(
            lhs[:, (2 - dy) * 256:(2 - dy) * 256 + RUN * 512],
            srun[...].reshape(RUN * 512, 128), preferred_element_type=F32,
        ).astype(BF16)
        for i in range(9):
            t = dy * 9 + i
            kgc[t // TILES, t % TILES] = block[i * SHARE:(i + 1) * SHARE]
    kgc[WIDE - 1, TILES - 1] = split(jnp.sum(bias, axis=1, keepdims=True)).astype(BF16)

    def rs_out(d):
        return remote(
            kgc.at[lax.div(peer(d), 2)], rsb.at[g], rs_send.at[d], rs_recv.at[d], sec, peer(d) * RUN + y
        )

    def rs_in(d):
        return remote(
            kgc.at[0], rsb.at[peer_in(d)], rs_send.at[d], rs_recv.at[d], sec, peer_in(d) * RUN + y
        )

    for d in range(1, GROUPS):
        rs_out(d).start()
    rsb[g] = kgc[x]

    def beside(d):
        return lax.rem(x + d, WIDE)

    def beside_in(d):
        return lax.rem(x + WIDE - d, WIDE)

    def across(at):
        return (2 * at + high) * RUN + y

    def a1_out(d):
        part = a1.at[y, x]
        return remote(part, part, a1_send.at[d], a1_recv.at[d], sec, across(beside(d)))

    def a1_in(d):
        part = a1.at[y, beside_in(d)]
        return remote(part, part, a1_send.at[d], a1_recv.at[d], sec, across(beside_in(d)))

    def b1_out(d):
        return remote(a1.at[y], a1.at[y], b1_send.at[d], b1_recv.at[d], sec, g * RUN + mate(d))

    def b1_in(d):
        part = a1.at[mate_in(d)]
        return remote(part, part, b1_send.at[d], b1_recv.at[d], sec, g * RUN + mate_in(d))

    def a2_out(d):
        part = a2.at[x, y]
        return remote(part, part, a2_send.at[d], a2_recv.at[d], sec, g * RUN + mate(d))

    def a2_in(d):
        part = a2.at[x, mate_in(d)]
        return remote(part, part, a2_send.at[d], a2_recv.at[d], sec, g * RUN + mate_in(d))

    def b2_out(d):
        return remote(a2.at[x], a2.at[x], b2_send.at[d], b2_recv.at[d], sec, across(beside(d)))

    def b2_in(d):
        part = a2.at[beside_in(d)]
        return remote(part, part, b2_send.at[d], b2_recv.at[d], sec, across(beside_in(d)))

    for d in range(1, GROUPS):
        rs_in(d).wait_recv()
    total = rsb[0].astype(F32)
    for d in range(1, GROUPS):
        total = total + rsb[d].astype(F32)
    final = total[TILES - 1]
    pair = split(final[:, 0:1] + final[:, 1:2])
    a1[y, x] = total[:AHEAD].astype(BF16)
    a2[x, y, 0:TILES - 1 - AHEAD] = total[AHEAD:TILES - 1].astype(BF16)
    a2[x, y, TILES - 1 - AHEAD] = jnp.where(x == WIDE - 1, pair, final).astype(BF16)
    for d in range(1, WIDE):
        a1_out(d).start()
    for d in range(1, RUN):
        a2_out(d).start()
    act_ref[...] = act6[2:4]
    for d in range(1, WIDE):
        a1_in(d).wait_recv()
    for d in range(1, RUN):
        b1_out(d).start()
    for d in range(1, RUN):
        a2_in(d).wait_recv()
    for d in range(1, WIDE):
        b2_out(d).start()

    @when(has_low)
    def _():
        halo(True).wait_send()

    @when(has_high)
    def _():
        halo(False).wait_send()

    for step in range(4):
        up_out(step).wait_send()
        if step < 3:
            down_out(step).wait_send()

    @when(odd)
    def _():
        for r in range(1, 5):
            to_sibling(r).wait_send()

    @when(sec >= 4, odd)
    def _():
        to_skip(4).wait_send()

    @when(sec >= 4, even)
    def _():
        to_skip(2).wait_send()

    for i in range(2):
        @when(has_end[i])
        def _():
            for d in range(1, RUN):
                end_out(i, d).wait_send()

    for d in range(1, RUN):
        mx_out(d).wait_send()
        rs_out(d).wait_send()
        a2_out(d).wait_send()
        b1_out(d).wait_send()
    for d in range(1, WIDE):
        a1_out(d).wait_send()
        b2_out(d).wait_send()
        b2_in(d).wait_recv()
    for d in range(1, RUN):
        b1_in(d).wait_recv()


def finish(norm_factor, act_in, a1, a2, act_ref, kg_ref, bias_ref):
    act_ref[0] = act_in[...].reshape(act_ref.shape[1:])
    for t in range(WIDE * TILES):
        q, i = t // TILES, t % TILES
        if i < AHEAD:
            tile = a1[:, q, i]
        else:
            tile = a2[q, :, i - AHEAD]
        tile = tile.reshape(128, 128).astype(F32).T * norm_factor
        if t < 27:
            kg_ref[0, t] = tile
        else:
            bias_ref[...] = tile[0:1] + tile[1:2]


def local(saved_in, saved_out, weights, cotangent):
    rows_y, cells_x, cells_z, channels = cotangent.shape
    norm_factor = 1.0 / math.sqrt(rows_y * lax.axis_size("slab") * cells_x * cells_z)
    flat = (rows_y, cells_x * cells_z, channels)
    vmem = pl.BlockSpec(memory_space=pltpu.VMEM)
    hbm = pl.BlockSpec(memory_space=pl.ANY)
    six = pltpu.VMEM((6, 256, 128), BF16)
    two = pltpu.VMEM((2, 256, 128), BF16)
    sems = pltpu.SemaphoreType.DMA
    act, a1, a2 = pl.pallas_call(
        kernel,
        name="backward",
        out_shape=(
            jax.ShapeDtypeStruct(flat, BF16),
            jax.ShapeDtypeStruct((RUN, WIDE, AHEAD, SHARE, channels), BF16),
            jax.ShapeDtypeStruct((WIDE, RUN, TILES - AHEAD, SHARE, channels), BF16),
        ),
        in_specs=[hbm] * 4,
        out_specs=(vmem,) * 3,
        scratch_shapes=[
            pltpu.VMEM((27, 128, 128), BF16), two, two,
            six, six, six, six,
            pltpu.VMEM((6, 256, 1152), BF16),
            pltpu.VMEM((1152, 384), BF16),
            pltpu.VMEM((RUN, SHARE, 512), BF16),
            pltpu.VMEM((RUN, SHARE, 256), BF16),
            pltpu.VMEM((RUN, SHARE, 512), BF16),
            pltpu.VMEM((2, SHARE, 256), BF16),
            pltpu.VMEM((9 * SHARE, RUN * 512 + 512), BF16),
            pltpu.VMEM((2 * RUN, 256, 128), BF16),
            pltpu.VMEM((WIDE, TILES, SHARE, 128), BF16),
            pltpu.VMEM((GROUPS, TILES, SHARE, 128), BF16),
            sems((4,)), sems((2,)), sems((2,)),
            sems((4,)), sems((4,)), sems((6,)), sems((6,)), sems, sems((2,)),
            pltpu.SemaphoreType.REGULAR,
            sems((4,)), sems((4,)), sems((3,)), sems((3,)), sems((8,)), sems((2,)),
            sems((8,)), sems((8,)), sems((8,)), sems((8,)),
            sems((8,)), sems((8,)), sems((8,)), sems((8,)),
            sems((8,)), sems((8,)), sems((8,)), sems((8,)),
        ],
        compiler_params=pltpu.CompilerParams(
            collective_id=0, has_side_effects=True, vmem_limit_bytes=56 << 20
        ),
    )(
        saved_in[0].reshape(flat), saved_out[0].reshape(flat), weights[0], cotangent.reshape(flat)
    )
    return pl.pallas_call(
        functools.partial(finish, norm_factor),
        name="finish",
        out_shape=(
            jax.ShapeDtypeStruct((1,) + cotangent.shape, BF16),
            jax.ShapeDtypeStruct((1, 27, channels, channels), F32),
            jax.ShapeDtypeStruct((1, channels), F32),
        ),
        in_specs=[vmem] * 3,
        out_specs=(vmem,) * 3,
    )(act, a1, a2)


def solution(mesh):
    placed = (
        P("section", "slab", None, None, None),
        P("section", "slab", None, None, None),
        P("section", None, None, None),
        P("slab", None, None, None),
    )
    return jax.shard_map(
        local,
        mesh=mesh,
        in_specs=placed,
        out_specs=(
            P("section", "slab", None, None, None),
            P("section", None, None, None),
            P("section", None),
        ),
        check_vma=False,
    )
```

time: 113 us -> 92.6 us (0.82)
  the two profiles are of different devices: /device:TPU:8 before, /device:TPU:16 now
where the time goes in v3:
time: 92.6 us; the launch traced here: 92.4 us
  Pallas kernels  91.8 us (99%)
    pallas_call x1, Pallas kernels, local(): pl.pallas_call(kernel, name='backward', out_shape=(jax.ShapeDtypeStruct(f...  89 us
    pallas_call x1, Pallas kernels, local(): pl.pallas_call(functools.partial(finish, norm_factor), name='finish', out...  2.75 us

profile of v3, /device:TPU:16, one launch (start us, length us, event | category | flops | bytes accessed | tf_op | source)
XLA Modules:
  0.0 92.4 jit_solution(3214631023588802020)
XLA Ops:
  0.6 89.0 %backward.1 = (bf16[2,256,128]{2,1,0:T(8,128)(2,1)}, bf16[8,4,2,16,128]{4,3,2,1,0:T(8,128)(2,1)}, bf16[4,8,5,16,128]{4,3,2,1,0:T(8,128)(2,1)}) custom-call(bf16[2,256,128]{2,1,0:T(8,128)(2,1)} %bitcast.5, bf16[2,256,128]{2,1,0:T(8,128)(2,1)} %bitcast.6, bf16[27,128,128]{2,1,0:T(8,128)(2,1)} %bitcast.4, bf16[2,256,128]{2,1,0:T(8,128)(2,1)} %bitcast.7), custom_call_target="tpu_custom_call" | custom-call | tf_op jit(solution)/shard_map/backward/pallas_call | solution.py:651
  89.7 2.8 %finish.1 = (bf16[1,2,32,8,128]{4,3,2,1,0:T(8,128)(2,1)}, f32[1,27,128,128]{3,2,1,0:T(8,128)}, f32[1,128]{1,0:T(1,128)}) custom-call(bf16[2,256,128]{2,1,0:T(8,128)(2,1)} %get-tuple-element.6.act_in, bf16[8,4,2,16,128]{4,3,2,1,0:T(8,128)(2,1)} %get-tuple-element.7.a1, bf16[4,8,5,16,128]{4,3,2,1,0:T(8,128)(2,1)} %get-tuple-element.8.a2), custom_call_target="tpu_custom_call" | custom-call | tf_op jit(solution)/shard_map/finish/pallas_call | solution.py:688

commit v4 on v3

--- a/solution.py
+++ b/solution.py
@@ -23,8 +23,9 @@
 def kernel(
     si_ref, so_ref, w_ref, cot_ref,
     act_ref, a1, a2,
-    wv, sov, cotv, inc, so6, act6, skip6, s9, w9, mt, mtx, mrun, ends, lhs, srun, kgc, rsb,
-    load, halo_send, halo_recv, row_send, row_recv, slab_send, slab_recv, skip_send, skip_recv, go,
+    wv, sov, cotv, inc, so6, act6, skip6, s9, w9, sob, act6b, skip6b, s9b, w9b, mt, mtx, mrun, ends, lhs, srun, kgc, rsb,
+    load, halo_send, halo_recv, row_send, row_recv, slab_send, slab_recv, skip_send, skip_recv,
+    pair_send, pair_recv, skip_send_b, skip_recv_b, go,
     up_send, up_recv, down_send, down_recv, end_send, end_recv,
     mx_send, mx_recv, rs_send, rs_recv,
     a1_send, a1_recv, b1_send, b1_recv, a2_send, a2_recv, b2_send, b2_recv,
@@ -59,7 +60,7 @@
             pltpu.make_async_copy(so_ref, sov, load.at[0]),
             pltpu.make_async_copy(cot_ref, cotv, load.at[1]),
             pltpu.make_async_copy(w_ref, wv, load.at[2]),
-            pltpu.make_async_copy(si_ref, srun.at[pl.ds(2 * y, 2)], load.at[3]),
+            pltpu.make_async_copy(si_ref, srun.at[pl.ds(1 + 2 * y, 2)], load.at[3]),
         )
 
     for c in loads():
@@ -91,21 +92,18 @@
     def _():
         signal(sec + 1, j)
 
-    @when(even, sec > 0, has_low)
-    def _():
-        signal(sec - 1, j - 1)
-
-    @when(even, sec > 0, has_high)
-    def _():
-        signal(sec - 1, j + 1)
-
-    @when(odd, jnp.logical_not(top), has_low)
-    def _():
-        signal(sec + 1, j - 1)
-
-    @when(odd, jnp.logical_not(top), has_high)
-    def _():
-        signal(sec + 1, j + 1)
+    for step, there in ((-2, both(odd, sec > 1)), (2, both(odd, jnp.logical_not(top)))):
+        @when(there)
+        def _():
+            signal(sec + step, j)
+
+        @when(there, has_low)
+        def _():
+            signal(sec + step, j - 1)
+
+        @when(there, has_high)
+        def _():
+            signal(sec + step, j + 1)
 
     @when(sec >= 4)
     def _():
@@ -118,12 +116,12 @@
     def one(*conditions):
         return jnp.where(both(*conditions), 1, 0)
 
-    diagonal = jnp.logical_or(both(even, sec > 0), both(odd, jnp.logical_not(top)))
+    pairs = one(odd, sec > 1) + one(odd, jnp.logical_not(top))
     expected = (
         RUN - 1 + GROUPS - 1 + 1
         + one(has_low, first) + one(has_high, last)
         + one(sec > 0) + one(jnp.logical_not(top))
-        + one(diagonal, has_low) + one(diagonal, has_high)
+        + pairs * (1 + one(has_low) + one(has_high))
     )
 
     blank = jnp.zeros((2, 256, 128), BF16)
@@ -143,6 +141,9 @@
         @when(odd)
         def _():
             inc[4:6] = blank
+
+    srun[0] = blank[0]
+    srun[2 * RUN + 1] = blank[0]
 
     @when(g == 0)
     def _():
@@ -163,6 +164,30 @@
     @when(jnp.logical_not(top))
     def _():
         so6[2:4] = sov[...]
+
+    load_si.wait()
+
+    pl.semaphore_wait(barrier, expected)
+
+    def remote(src, dst, ss, rs, s, t):
+        return pltpu.make_async_remote_copy(
+            src_ref=src, dst_ref=dst, send_sem=ss, recv_sem=rs,
+            device_id=(s, t), device_id_type=MESH,
+        )
+
+    def halo(low):
+        own = so6.at[2:4]
+        if low:
+            return remote(own, so6.at[4:6], halo_send.at[0], halo_recv.at[0], sec, j - 1)
+        return remote(own, so6.at[0:2], halo_send.at[1], halo_recv.at[1], sec, j + 1)
+
+    @when(has_low)
+    def _():
+        halo(True).start()
+
+    @when(has_high)
+    def _():
+        halo(False).start()
 
     load_w.wait()
 
@@ -174,29 +199,14 @@
         return carry
 
     lax.fori_loop(0, 27, turn, 0)
-    load_si.wait()
-
-    pl.semaphore_wait(barrier, expected)
-
-    def remote(src, dst, ss, rs, s, t):
-        return pltpu.make_async_remote_copy(
-            src_ref=src, dst_ref=dst, send_sem=ss, recv_sem=rs,
-            device_id=(s, t), device_id_type=MESH,
-        )
-
-    def halo(low):
-        own = so6.at[2:4]
-        if low:
-            return remote(own, so6.at[4:6], halo_send.at[0], halo_recv.at[0], sec, j - 1)
-        return remote(own, so6.at[0:2], halo_send.at[1], halo_recv.at[1], sec, j + 1)
-
-    @when(has_low)
-    def _():
-        halo(True).start()
-
-    @when(has_high)
-    def _():
-        halo(False).start()
+    def to_pair(i):
+        if i == 0:
+            return remote(w9, w9b, pair_send.at[0], pair_recv.at[0], sec + 1, j)
+        return remote(so6.at[1:5], sob.at[1:5], pair_send.at[1], pair_recv.at[1], sec + 1, j)
+
+    @when(even, sec > 0)
+    def _():
+        to_pair(0).start()
 
     def mate(d):
         return lax.rem(y + d, RUN)
@@ -211,7 +221,7 @@
         return lax.rem(g + GROUPS - d, GROUPS)
 
     def rows_of(origin):
-        return srun.at[pl.ds(2 * origin, 2)]
+        return srun.at[pl.ds(1 + 2 * origin, 2)]
 
     def up_out(step):
         rows = rows_of(lax.rem(y + RUN - step, RUN))
@@ -232,8 +242,8 @@
     low_row = g > 0
     high_row = g < GROUPS - 1
 
-    def gather_run():
-        for step in range(4):
+    def gather_run(steps):
+        for step in steps:
             up_out(step).start()
             if step < 3:
                 down_out(step).start()
@@ -251,12 +261,22 @@
             def _():
                 halo(True).wait_recv()
 
-    early = sec < n_sec - 2
-    late = sec >= n_sec - 2
-
-    @when(early)
-    def _():
-        gather_run()
+    @when(even)
+    def _():
+        halo_wait(True)
+        halo_wait(False)
+
+    @when(even, sec > 0)
+    def _():
+        to_pair(1).start()
+
+    @when(sec < n_sec - 2)
+    def _():
+        gather_run((0, 1))
+
+    @when(sec < n_sec // 2)
+    def _():
+        gather_run((2, 3))
 
     def to_sibling(r):
         return remote(act6.at[r], inc.at[r], row_send.at[r - 1], row_recv.at[r - 1], sec - 1, j)
@@ -265,7 +285,7 @@
         at = (2, 4, 0)[which] + i
         k = 3 * i + which
         return remote(
-            act6.at[2 + i], inc.at[at], slab_send.at[k], slab_recv.at[k], sec - 1, j + (0, -1, 1)[which]
+            act6b.at[2 + i], inc.at[at], slab_send.at[k], slab_recv.at[k], sec - 2, j + (0, -1, 1)[which]
         )
 
     def slab_sends(i, act):
@@ -284,13 +304,24 @@
             return remote(act6.at[1:5], skip6.at[1:5], skip_send, skip_recv.at[0], sec - 4, j)
         return remote(act6.at[2:4], skip6.at[2:4], skip_send, skip_recv.at[1], sec - 4, j)
 
+    def to_skip_b():
+        return remote(act6b.at[2:4], skip6b.at[2:4], skip_send_b, skip_recv_b, sec - 4, j)
+
     depth = lax.broadcasted_iota(jnp.int32, (32, 8, 128), 1)
     edge_x = jnp.zeros((8, 128), F32)
 
     def stack_row(r, carry):
         held = so6[r].astype(F32)
         arrived = jnp.where(held > 0, inc[r].astype(F32), 0.0)
-        m = jnp.where(top, held, arrived).reshape(32, 8, 128)
+        put_row(s9, r, jnp.where(top, held, arrived))
+        return carry
+
+    def stack_pair(r, carry):
+        put_row(s9b, r, jnp.where(sob[r].astype(F32) > 0, act6[r].astype(F32), 0.0))
+        return carry
+
+    def put_row(s9, r, m):
+        m = m.reshape(32, 8, 128)
         up = jnp.where(depth == 7, 0.0, pltpu.roll(m, 7, 1)).reshape(256, 128)
         down = jnp.where(depth == 0, 0.0, pltpu.roll(m, 1, 1)).reshape(256, 128)
         for b, v in enumerate((up, m.reshape(256, 128), down)):
@@ -298,9 +329,12 @@
             s9[r, :, at:at + 128] = jnp.concatenate([v[8:], edge_x], 0).astype(BF16)
             s9[r, :, at + 384:at + 512] = v.astype(BF16)
             s9[r, :, at + 768:at + 896] = jnp.concatenate([edge_x, v[:-8]], 0).astype(BF16)
-        return carry
-
-    def layer(lo, hi, steps, done):
+
+    mine = (s9, w9, skip6, act6)
+    pair = (s9b, w9b, skip6b, act6b)
+
+    def layer(refs, lo, hi, steps, done):
+        s9, w9, skip6, act6 = refs
         sums, count = {}, {}
         for ready, rows in steps:
             ready()
@@ -348,7 +382,23 @@
         lows = (lambda: side(True), (0, 1))
         highs = (lambda: side(False), (4, 5))
         order = [lows, highs] if low_first else [highs, lows]
-        layer(1, 5, [(own, (2, 3))] + order, lambda r: to_sibling(r).start())
+        layer(mine, 1, 5, [(own, (2, 3))] + order, lambda r: to_sibling(r).start())
+
+        @when(sec > 1)
+        def _():
+            to_pair(0).wait_recv()
+            to_pair(1).wait_recv()
+
+            @when(sec < 4)
+            def _():
+                to_skip_b().wait_recv()
+
+            rows = (1, 2, 3, 4) if low_first else (4, 3, 2, 1)
+            layer(
+                pair, 2, 4,
+                [(lambda r=r: lax.fori_loop(r, r + 1, stack_pair, 0), (r,)) for r in rows],
+                lambda r: slab_sends(r - 2, "start"),
+            )
 
     def even_layer(low_first):
         rows = (1, 2, 3, 4) if low_first else (4, 3, 2, 1)
@@ -361,10 +411,7 @@
         def _():
             to_skip(2).wait_recv()
 
-        layer(
-            2, 4, [(lambda r=r: ready(r), (r,)) for r in rows],
-            lambda r: slab_sends(r - 2, "start"),
-        )
+        layer(mine, 2, 4, [(lambda r=r: ready(r), (r,)) for r in rows], lambda r: None)
 
     @when(odd, first)
     def _():
@@ -374,11 +421,6 @@
     def _():
         odd_layer(True)
 
-    @when(even)
-    def _():
-        halo_wait(True)
-        halo_wait(False)
-
     @when(even, sec > 0, first)
     def _():
         even_layer(False)
@@ -389,9 +431,9 @@
 
     @when(sec == 0)
     def _():
-        for r in range(1, 5):
+        for r in (2, 3):
             to_sibling(r).wait_recv()
-        lax.fori_loop(1, 5, stack_row, 0)
+        lax.fori_loop(2, 4, stack_row, 0)
 
     def turned(r, h):
         block = s9[r, h * 128:(h + 1) * 128, 512:640].astype(F32).T.astype(BF16)
@@ -402,21 +444,19 @@
             at = r * 256 + h * 128
             mt[:, :, at:at + 128] = turned(2 + r, h)
 
-    for outer, r in ((both(first, low_row), 1), (both(last, high_row), 4)):
-        @when(outer)
-        def _():
-            for h in range(2):
-                mtx[:, :, h * 128:(h + 1) * 128] = turned(r, h)
-
-    @when(even, sec > 0)
+    @when(odd, sec > 1)
     def _():
         slab_sends(0, "wait_send")
         slab_sends(1, "wait_send")
-        pl.semaphore_signal(go, inc=1, device_id=(sec + 1, j), device_id_type=MESH)
-
-    @when(odd, sec > 1)
+        pl.semaphore_signal(go, inc=1, device_id=(sec - 1, j), device_id_type=MESH)
+
+    @when(even, sec > 0)
     def _():
         pl.semaphore_wait(go, 1)
+
+    @when(top)
+    def _():
+        to_skip_b().start()
 
     @when(sec >= 4, odd)
     def _():
@@ -439,6 +479,18 @@
         mx_out(d).start()
     mrun[y] = mt[y]
 
+    @when(sec == 0)
+    def _():
+        for r in (1, 4):
+            to_sibling(r).wait_recv()
+            lax.fori_loop(r, r + 1, stack_row, 0)
+
+    for outer, r in ((both(first, low_row), 1), (both(last, high_row), 4)):
+        @when(outer)
+        def _():
+            for h in range(2):
+                mtx[:, :, h * 128:(h + 1) * 128] = turned(r, h)
+
     has_end = (both(first, low_row), both(last, high_row))
     for i in range(2):
         @when(has_end[i])
@@ -450,11 +502,15 @@
     @when(sec == 0)
     def _():
         to_skip(2).wait_recv()
-        layer(2, 4, [(lambda: None, (1, 2, 3, 4))], lambda r: None)
-
-    @when(late)
-    def _():
-        gather_run()
+        layer(mine, 2, 4, [(lambda: None, (1, 2, 3, 4))], lambda r: None)
+
+    @when(sec >= n_sec - 2)
+    def _():
+        gather_run((0, 1))
+
+    @when(sec >= n_sec // 2)
+    def _():
+        gather_run((2, 3))
 
     lane = lax.broadcasted_iota(jnp.int32, (SHARE, 512), 1)
     cell_x = lax.rem(lax.div(lane, 8), 32)
@@ -464,27 +520,35 @@
         for dz in (-1, 0, 1):
             fits.append(both(cell_x - dx >= 0, cell_x - dx < 32, cell_z - dz >= 0, cell_z - dz < 8))
 
-    for d in range(1, RUN):
-        mx_in(d).wait_recv()
-
-    for i, (there, away) in enumerate(((low_row, y > 0), (high_row, y < RUN - 1))):
-        @when(there, away)
-        def _():
-            end_out(i, 1).wait_recv()
-
-    def spread(m, at, width):
+    def spread(m, slot, width):
         for i, ok in enumerate(fits):
             step = ((i // 3 - 1) * 8 + i % 3 - 1) % width
             moved = m if step == 0 else jnp.where(ok[:, :width], pltpu.roll(m, step, 1), 0.0)
-            lhs[i * SHARE:(i + 1) * SHARE, at:at + width] = moved.astype(BF16)
+            lhs[slot, i * SHARE:(i + 1) * SHARE, 0:width] = moved.astype(BF16)
 
     bias = jnp.zeros((SHARE, 512), F32)
-    spread(ends[0].astype(F32), 0, 256)
-    for u in range(RUN):
+    terms = [jnp.zeros((9 * SHARE, 128), F32)] * 3
+    for n, d in enumerate((0, 1, 7, 2, 6, 3, 5, 4)):
+        if d > 0:
+            mx_in(d).wait_recv()
+        u = mate_in(d)
         m = mrun[u].astype(F32)
         bias = bias + m
-        spread(m, 256 + u * 512, 512)
-    spread(ends[1].astype(F32), 256 + RUN * 512, 256)
+        spread(m, n, 512)
+        for dy in range(3):
+            terms[dy] = terms[dy] + jnp.dot(
+                lhs[n], srun[pl.ds(2 * u + dy, 2)].reshape(512, 128), preferred_element_type=F32
+            )
+    for i, (there, away) in enumerate(((low_row, y > 0), (high_row, y < RUN - 1))):
+        @when(there, away)
+        def _():
+            end_out(i, 1).wait_recv()
+
+        spread(ends[i].astype(F32), RUN + i, 256)
+        dy, row = ((2, 1), (0, 2 * RUN))[i]
+        terms[dy] = terms[dy] + jnp.dot(
+            lhs[RUN + i, :, 0:256], srun[row], preferred_element_type=F32
+        )
 
     column = lax.broadcasted_iota(jnp.int32, (SHARE, 128), 1)
 
@@ -493,10 +557,7 @@
         return jnp.where(column == 0, head, jnp.where(column == 1, total - head, 0.0))
 
     for dy in range(3):
-        block = jnp.dot(
-            lhs[:, (2 - dy) * 256:(2 - dy) * 256 + RUN * 512],
-            srun[...].reshape(RUN * 512, 128), preferred_element_type=F32,
-        ).astype(BF16)
+        block = terms[dy].astype(BF16)
         for i in range(9):
             t = dy * 9 + i
             kgc[t // TILES, t % TILES] = block[i * SHARE:(i + 1) * SHARE]
@@ -597,6 +658,15 @@
         for r in range(1, 5):
             to_sibling(r).wait_send()
 
+    @when(even, sec > 0)
+    def _():
+        to_pair(0).wait_send()
+        to_pair(1).wait_send()
+
+    @when(top)
+    def _():
+        to_skip_b().wait_send()
+
     @when(sec >= 4, odd)
     def _():
         to_skip(4).wait_send()
@@ -628,10 +698,7 @@
     act_ref[0] = act_in[...].reshape(act_ref.shape[1:])
     for t in range(WIDE * TILES):
         q, i = t // TILES, t % TILES
-        if i < AHEAD:
-            tile = a1[:, q, i]
-        else:
-            tile = a2[q, :, i - AHEAD]
+        tile = a1[:, q, i] if i < AHEAD else a2[q, :, i - AHEAD]
         tile = tile.reshape(128, 128).astype(F32).T * norm_factor
         if t < 27:
             kg_ref[0, t] = tile
@@ -663,16 +730,20 @@
             six, six, six, six,
             pltpu.VMEM((6, 256, 1152), BF16),
             pltpu.VMEM((1152, 384), BF16),
+            six, six, six,
+            pltpu.VMEM((6, 256, 1152), BF16),
+            pltpu.VMEM((1152, 384), BF16),
             pltpu.VMEM((RUN, SHARE, 512), BF16),
             pltpu.VMEM((RUN, SHARE, 256), BF16),
             pltpu.VMEM((RUN, SHARE, 512), BF16),
             pltpu.VMEM((2, SHARE, 256), BF16),
-            pltpu.VMEM((9 * SHARE, RUN * 512 + 512), BF16),
-            pltpu.VMEM((2 * RUN, 256, 128), BF16),
+            pltpu.VMEM((RUN + 2, 9 * SHARE, 512), BF16),
+            pltpu.VMEM((2 * RUN + 2, 256, 128), BF16),
             pltpu.VMEM((WIDE, TILES, SHARE, 128), BF16),
             pltpu.VMEM((GROUPS, TILES, SHARE, 128), BF16),
             sems((4,)), sems((2,)), sems((2,)),
             sems((4,)), sems((4,)), sems((6,)), sems((6,)), sems, sems((2,)),
+            sems((2,)), sems((2,)), sems, sems,
             pltpu.SemaphoreType.REGULAR,
             sems((4,)), sems((4,)), sems((3,)), sems((3,)), sems((8,)), sems((2,)),
             sems((8,)), sems((8,)), sems((8,)), sems((8,)),

time: 92.6 us -> 86.3 us (0.932)
  the two profiles are of different devices: /device:TPU:16 before, /device:TPU:4 now
where the time goes in v4:
time: 86.3 us; the launch traced here: 86.2 us
  Pallas kernels  85.5 us (99%)
    pallas_call x1, Pallas kernels, local(): pl.pallas_call(kernel, name='backward', out_shape=(jax.ShapeDtypeStruct(f...  82.8 us
    pallas_call x1, Pallas kernels, local(): pl.pallas_call(functools.partial(finish, norm_factor), name='finish', out...  2.75 us

profile of v4, /device:TPU:4, one launch (start us, length us, event | category | flops | bytes accessed | tf_op | source)
XLA Modules:
  0.0 86.2 jit_solution(3762106192133482685)
XLA Ops:
  0.6 82.8 %backward.1 = (bf16[2,256,128]{2,1,0:T(8,128)(2,1)}, bf16[8,4,2,16,128]{4,3,2,1,0:T(8,128)(2,1)}, bf16[4,8,5,16,128]{4,3,2,1,0:T(8,128)(2,1)}) custom-call(bf16[2,256,128]{2,1,0:T(8,128)(2,1)} %bitcast.5, bf16[2,256,128]{2,1,0:T(8,128)(2,1)} %bitcast.6, bf16[27,128,128]{2,1,0:T(8,128)(2,1)} %bitcast.4, bf16[2,256,128]{2,1,0:T(8,128)(2,1)} %bitcast.7), custom_call_target="tpu_custom_call" | custom-call | tf_op jit(solution)/shard_map/backward/pallas_call | solution.py:718
  83.4 2.8 %finish.1 = (bf16[1,2,32,8,128]{4,3,2,1,0:T(8,128)(2,1)}, f32[1,27,128,128]{3,2,1,0:T(8,128)}, f32[1,128]{1,0:T(1,128)}) custom-call(bf16[2,256,128]{2,1,0:T(8,128)(2,1)} %get-tuple-element.6.act_in, bf16[8,4,2,16,128]{4,3,2,1,0:T(8,128)(2,1)} %get-tuple-element.7.a1, bf16[4,8,5,16,128]{4,3,2,1,0:T(8,128)(2,1)} %get-tuple-element.8.a2), custom_call_target="tpu_custom_call" | custom-call | tf_op jit(solution)/shard_map/finish/pallas_call | solution.py:759

commit v5 on v4

--- a/solution.py
+++ b/solution.py
@@ -17,6 +17,8 @@
 SHARE = 16
 WIDE = 4
 TILES = 7
+FAR = (4, 3, 5, 2, 6, 1, 7)
+FAR_RUNS = (3, 5, 1, 7, 4, 2, 6)
 AHEAD = 2
 
 
@@ -475,7 +477,7 @@
     def end_out(i, d):
         return remote(mtx.at[mate(d)], ends.at[i], end_send.at[d], end_recv.at[i], sec, g * RUN + mate(d))
 
-    for d in range(1, RUN):
+    for d in FAR:
         mx_out(d).start()
     mrun[y] = mt[y]
 
@@ -498,11 +500,6 @@
             for d in range(1, RUN):
                 end_out(i, d).start()
             ends[i] = mtx[y]
-
-    @when(sec == 0)
-    def _():
-        to_skip(2).wait_recv()
-        layer(mine, 2, 4, [(lambda: None, (1, 2, 3, 4))], lambda r: None)
 
     @when(sec >= n_sec - 2)
     def _():
@@ -573,9 +570,14 @@
             kgc.at[0], rsb.at[peer_in(d)], rs_send.at[d], rs_recv.at[d], sec, peer_in(d) * RUN + y
         )
 
-    for d in range(1, GROUPS):
+    for d in FAR_RUNS:
         rs_out(d).start()
     rsb[g] = kgc[x]
+
+    @when(sec == 0)
+    def _():
+        to_skip(2).wait_recv()
+        layer(mine, 2, 4, [(lambda: None, (1, 2, 3, 4))], lambda r: None)
 
     def beside(d):
         return lax.rem(x + d, WIDE)
@@ -628,12 +630,12 @@
     a2[x, y, TILES - 1 - AHEAD] = jnp.where(x == WIDE - 1, pair, final).astype(BF16)
     for d in range(1, WIDE):
         a1_out(d).start()
-    for d in range(1, RUN):
+    for d in FAR:
         a2_out(d).start()
-    act_ref[...] = act6[2:4]
+    act_ref[...] = act6[2:4].reshape(act_ref.shape)
     for d in range(1, WIDE):
         a1_in(d).wait_recv()
-    for d in range(1, RUN):
+    for d in FAR:
         b1_out(d).start()
     for d in range(1, RUN):
         a2_in(d).wait_recv()
@@ -695,7 +697,7 @@
 
 
 def finish(norm_factor, act_in, a1, a2, act_ref, kg_ref, bias_ref):
-    act_ref[0] = act_in[...].reshape(act_ref.shape[1:])
+    act_ref[...] = act_in[...]
     for t in range(WIDE * TILES):
         q, i = t // TILES, t % TILES
         tile = a1[:, q, i] if i < AHEAD else a2[q, :, i - AHEAD]
@@ -719,7 +721,7 @@
         kernel,
         name="backward",
         out_shape=(
-            jax.ShapeDtypeStruct(flat, BF16),
+            jax.ShapeDtypeStruct((1,) + cotangent.shape, BF16),
             jax.ShapeDtypeStruct((RUN, WIDE, AHEAD, SHARE, channels), BF16),
             jax.ShapeDtypeStruct((WIDE, RUN, TILES - AHEAD, SHARE, channels), BF16),
         ),

time: 86.3 us -> 84.7 us (0.981)
  the two profiles are of different devices: /device:TPU:4 before, /device:TPU:8 now
where the time goes in v5:
time: 84.7 us; the launch traced here: 84.5 us
  Pallas kernels  83.9 us (99%)
    pallas_call x1, Pallas kernels, local(): pl.pallas_call(kernel, name='backward', out_shape=(jax.ShapeDtypeStruct((...  81.2 us
    pallas_call x1, Pallas kernels, local(): pl.pallas_call(functools.partial(finish, norm_factor), name='finish', out...  2.75 us

profile of v5, /device:TPU:8, one launch (start us, length us, event | category | flops | bytes accessed | tf_op | source)
XLA Modules:
  0.0 84.5 jit_solution(3752126829185257594)
XLA Ops:
  0.6 81.2 %backward.1 = (bf16[1,2,32,8,128]{4,3,2,1,0:T(8,128)(2,1)}, bf16[8,4,2,16,128]{4,3,2,1,0:T(8,128)(2,1)}, bf16[4,8,5,16,128]{4,3,2,1,0:T(8,128)(2,1)}) custom-call(bf16[2,256,128]{2,1,0:T(8,128)(2,1)} %bitcast.5, bf16[2,256,128]{2,1,0:T(8,128)(2,1)} %bitcast.6, bf16[27,128,128]{2,1,0:T(8,128)(2,1)} %bitcast.4, bf16[2,256,128]{2,1,0:T(8,128)(2,1)} %bitcast.7), custom_call_target="tpu_custom_call" | custom-call | tf_op jit(solution)/shard_map/backward/pallas_call | solution.py:720
  81.8 2.8 %finish.1 = (bf16[1,2,32,8,128]{4,3,2,1,0:T(8,128)(2,1)}, f32[1,27,128,128]{3,2,1,0:T(8,128)}, f32[1,128]{1,0:T(1,128)}) custom-call(bf16[1,2,32,8,128]{4,3,2,1,0:T(8,128)(2,1)} %get-tuple-element.6.act_in, bf16[8,4,2,16,128]{4,3,2,1,0:T(8,128)(2,1)} %get-tuple-element.7.a1, bf16[4,8,5,16,128]{4,3,2,1,0:T(8,128)(2,1)} %get-tuple-element.8.a2), custom_call_target="tpu_custom_call" | custom-call | tf_op jit(solution)/shard_map/finish/pallas_call | solution.py:761

commit v6 on v5

--- a/solution.py
+++ b/solution.py
@@ -49,7 +49,7 @@
     high = lax.rem(g, 2)
 
     def both(*conditions):
-        out = conditions[0]
+        out = jnp.bool_(conditions[0]) if conditions[0] is True else conditions[0]
         for c in conditions[1:]:
             out = jnp.logical_and(out, c)
         return out
@@ -177,19 +177,24 @@
             device_id=(s, t), device_id_type=MESH,
         )
 
-    def halo(low):
-        own = so6.at[2:4]
+    def halo(low, rows):
         if low:
-            return remote(own, so6.at[4:6], halo_send.at[0], halo_recv.at[0], sec, j - 1)
-        return remote(own, so6.at[0:2], halo_send.at[1], halo_recv.at[1], sec, j + 1)
-
-    @when(has_low)
-    def _():
-        halo(True).start()
-
-    @when(has_high)
-    def _():
-        halo(False).start()
+            here, there = ((pl.ds(2, 2), pl.ds(4, 2)), (2, 4))[2 - rows]
+        else:
+            here, there = ((pl.ds(2, 2), pl.ds(0, 2)), (3, 1))[2 - rows]
+        i = 0 if low else 1
+        return remote(
+            so6.at[here], so6.at[there], halo_send.at[i], halo_recv.at[i], sec, j - 1 if low else j + 1
+        )
+
+    def halo_do(low, there, act):
+        for rows, parity in ((2, odd), (1, even)):
+            @when(there, parity)
+            def _():
+                getattr(halo(low, rows), act)()
+
+    halo_do(True, has_low, "start")
+    halo_do(False, has_high, "start")
 
     load_w.wait()
 
@@ -254,14 +259,7 @@
                 down_in(step).wait_recv()
 
     def halo_wait(low):
-        if low:
-            @when(has_low)
-            def _():
-                halo(False).wait_recv()
-        else:
-            @when(has_high)
-            def _():
-                halo(True).wait_recv()
+        halo_do(not low, has_low if low else has_high, "wait_recv")
 
     @when(even)
     def _():
@@ -290,16 +288,11 @@
             act6b.at[2 + i], inc.at[at], slab_send.at[k], slab_recv.at[k], sec - 2, j + (0, -1, 1)[which]
         )
 
-    def slab_sends(i, act):
-        getattr(to_slab(i, 0), act)()
-
-        @when(has_low)
-        def _():
-            getattr(to_slab(i, 1), act)()
-
-        @when(has_high)
-        def _():
-            getattr(to_slab(i, 2), act)()
+    def slab_sends(i, act, order=(1, 2, 0)):
+        for which in order:
+            @when((True, has_low, has_high)[which])
+            def _():
+                getattr(to_slab(i, which), act)()
 
     def to_skip(rows):
         if rows == 4:
@@ -399,7 +392,7 @@
             layer(
                 pair, 2, 4,
                 [(lambda r=r: lax.fori_loop(r, r + 1, stack_pair, 0), (r,)) for r in rows],
-                lambda r: slab_sends(r - 2, "start"),
+                lambda r: slab_sends(r - 2, "start", (2, 1, 0) if low_first else (1, 2, 0)),
             )
 
     def even_layer(low_first):
@@ -642,13 +635,8 @@
     for d in range(1, WIDE):
         b2_out(d).start()
 
-    @when(has_low)
-    def _():
-        halo(True).wait_send()
-
-    @when(has_high)
-    def _():
-        halo(False).wait_send()
+    halo_do(True, has_low, "wait_send")
+    halo_do(False, has_high, "wait_send")
 
     for step in range(4):
         up_out(step).wait_send()

time: 84.7 us -> 83.4 us (0.985)
  the two profiles are of different devices: /device:TPU:8 before, /device:TPU:4 now
where the time goes in v6:
time: 83.4 us; the launch traced here: 83.3 us
  Pallas kernels  82.6 us (99%)
    pallas_call x1, Pallas kernels, local(): pl.pallas_call(kernel, name='backward', out_shape=(jax.ShapeDtypeStruct((...  79.9 us
    pallas_call x1, Pallas kernels, local(): pl.pallas_call(functools.partial(finish, norm_factor), name='finish', out...  2.75 us

profile of v6, /device:TPU:4, one launch (start us, length us, event | category | flops | bytes accessed | tf_op | source)
XLA Modules:
  0.0 83.3 jit_solution(959916820162864571)
XLA Ops:
  0.6 79.9 %backward.1 = (bf16[1,2,32,8,128]{4,3,2,1,0:T(8,128)(2,1)}, bf16[8,4,2,16,128]{4,3,2,1,0:T(8,128)(2,1)}, bf16[4,8,5,16,128]{4,3,2,1,0:T(8,128)(2,1)}) custom-call(bf16[2,256,128]{2,1,0:T(8,128)(2,1)} %bitcast.5, bf16[2,256,128]{2,1,0:T(8,128)(2,1)} %bitcast.6, bf16[27,128,128]{2,1,0:T(8,128)(2,1)} %bitcast.4, bf16[2,256,128]{2,1,0:T(8,128)(2,1)} %bitcast.7), custom_call_target="tpu_custom_call" | custom-call | tf_op jit(solution)/shard_map/backward/pallas_call | solution.py:708
  80.5 2.8 %finish.1 = (bf16[1,2,32,8,128]{4,3,2,1,0:T(8,128)(2,1)}, f32[1,27,128,128]{3,2,1,0:T(8,128)}, f32[1,128]{1,0:T(1,128)}) custom-call(bf16[1,2,32,8,128]{4,3,2,1,0:T(8,128)(2,1)} %get-tuple-element.6.act_in, bf16[8,4,2,16,128]{4,3,2,1,0:T(8,128)(2,1)} %get-tuple-element.7.a1, bf16[4,8,5,16,128]{4,3,2,1,0:T(8,128)(2,1)} %get-tuple-element.8.a2), custom_call_target="tpu_custom_call" | custom-call | tf_op jit(solution)/shard_map/finish/pallas_call | solution.py:749

commit v7 on v6

--- a/solution.py
+++ b/solution.py
@@ -19,7 +19,7 @@
 TILES = 7
 FAR = (4, 3, 5, 2, 6, 1, 7)
 FAR_RUNS = (3, 5, 1, 7, 4, 2, 6)
-AHEAD = 2
+AHEAD = 3
 
 
 def kernel(

time: 83.4 us -> 83 us (level)
  the two profiles are of different devices: /device:TPU:4 before, /device:TPU:1 now
where the time goes in v7:
time: 83 us; the launch traced here: 82.9 us
  Pallas kernels  82.2 us (99%)
    pallas_call x1, Pallas kernels, local(): pl.pallas_call(kernel, name='backward', out_shape=(jax.ShapeDtypeStruct((...  79.5 us
    pallas_call x1, Pallas kernels, local(): pl.pallas_call(functools.partial(finish, norm_factor), name='finish', out...  2.74 us

profile of v7, /device:TPU:1, one launch (start us, length us, event | category | flops | bytes accessed | tf_op | source)
XLA Modules:
  0.0 82.9 jit_solution(747568540361216744)
XLA Ops:
  0.6 79.5 %backward.1 = (bf16[1,2,32,8,128]{4,3,2,1,0:T(8,128)(2,1)}, bf16[8,4,3,16,128]{4,3,2,1,0:T(8,128)(2,1)}, bf16[4,8,4,16,128]{4,3,2,1,0:T(8,128)(2,1)}) custom-call(bf16[2,256,128]{2,1,0:T(8,128)(2,1)} %bitcast.5, bf16[2,256,128]{2,1,0:T(8,128)(2,1)} %bitcast.6, bf16[27,128,128]{2,1,0:T(8,128)(2,1)} %bitcast.4, bf16[2,256,128]{2,1,0:T(8,128)(2,1)} %bitcast.7), custom_call_target="tpu_custom_call" | custom-call | tf_op jit(solution)/shard_map/backward/pallas_call | solution.py:708
  80.1 2.7 %finish.1 = (bf16[1,2,32,8,128]{4,3,2,1,0:T(8,128)(2,1)}, f32[1,27,128,128]{3,2,1,0:T(8,128)}, f32[1,128]{1,0:T(1,128)}) custom-call(bf16[1,2,32,8,128]{4,3,2,1,0:T(8,128)(2,1)} %get-tuple-element.6.act_in, bf16[8,4,3,16,128]{4,3,2,1,0:T(8,128)(2,1)} %get-tuple-element.7.a1, bf16[4,8,4,16,128]{4,3,2,1,0:T(8,128)(2,1)} %get-tuple-element.8.a2), custom_call_target="tpu_custom_call" | custom-call | tf_op jit(solution)/shard_map/finish/pallas_call | solution.py:749
